TPU v7x, 32 devices: a whole 2x2x4 slice. The times are simulated.
32 devices in a mesh: dp: 8 (over z, x), vocab: 4 (over y, core).
Axes of the slice: x: 2, y: 2, z: 4, core: 2. Of those that a mesh axis runs over, the one named last changes fastest.
Arguments:
- ids: int32 [8, 728], P('dp'), may hold values from 0 to 15359
- docs: int32 [8, 728], P('dp'), may hold values from 0 to 5, never falling along the last dimension, each value on 1 to 364 neighbouring positions
- resets: int32 [8, 1], P('dp'), may hold values 0 or 1
- mlm_pos: int32 [8, 112], P('dp'), may hold values from 0 to 727
- mlm_label: int32 [8, 112], P('dp'), may hold values from 0 to 15359
- step: int32 [1], replicated, may hold values from 2 to 20
- qkv_master: float32 [1, 768, 2304], P(None, 'dp'), may hold values from -0.21875 to 0.21875
- qkv_first: float32 [1, 768, 2304], P(None, 'dp'), may hold values from -7.6293945e-06 to 7.6293945e-06
- qkv_second: float32 [1, 768, 2304], P(None, 'dp'), may hold values from 2.0838335e-14 to 8.335334e-14
- out_master: float32 [1, 768, 768], P(None, 'dp'), may hold values from -0.625 to 0.625
- out_first: float32 [1, 768, 768], P(None, 'dp'), may hold values from -7.6293945e-06 to 7.6293945e-06
- out_second: float32 [1, 768, 768], P(None, 'dp'), may hold values from 2.0838335e-14 to 8.335334e-14
- up_master: float32 [1, 768, 3072], P(None, 'dp'), may hold values from -0.21875 to 0.21875
- up_first: float32 [1, 768, 3072], P(None, 'dp'), may hold values from -7.6293945e-06 to 7.6293945e-06
- up_second: float32 [1, 768, 3072], P(None, 'dp'), may hold values from 2.0838335e-14 to 8.335334e-14
- down_master: float32 [1, 3072, 768], P(None, 'dp'), may hold values from -0.109375 to 0.109375
- down_first: float32 [1, 3072, 768], P(None, 'dp'), may hold values from -7.6293945e-06 to 7.6293945e-06
- down_second: float32 [1, 3072, 768], P(None, 'dp'), may hold values from 2.0838335e-14 to 8.335334e-14
- embed_master: float32 [15360, 768], P(('dp', 'vocab')), may hold values from -0.42 to 0.42
- embed_first: float32 [15360, 768], P(('dp', 'vocab')), may hold values from -3.8146973e-06 to 3.8146973e-06
- embed_second: float32 [15360, 768], P(('dp', 'vocab')), may hold values from 5.209584e-15 to 2.0838335e-14
- vectors_master: float32 [1, 9216], replicated, may hold values from -1 to 1.2
- vectors_first: float32 [1, 9216], replicated, may hold values from -3.0517578e-05 to 3.0517578e-05
- vectors_second: float32 [1, 9216], replicated, may hold values from 3.3341336e-13 to 1.3336535e-12
- extras_master: float32 [406, 768], replicated, may hold values from -4 to 4
- extras_first: float32 [406, 768], replicated, may hold values from -1.5258789e-05 to 1.5258789e-05
- extras_second: float32 [406, 768], replicated, may hold values from 8.335334e-14 to 3.3341336e-13
Outputs:
- loss: float32 [], replicated
- grad_norm: float32 [], replicated
- qkv_new: float32 [1, 768, 2304], P(None, 'dp')
- qkv_first_new: float32 [1, 768, 2304], P(None, 'dp')
- qkv_second_new: float32 [1, 768, 2304], P(None, 'dp')
- out_new: float32 [1, 768, 768], P(None, 'dp')
- out_first_new: float32 [1, 768, 768], P(None, 'dp')
- out_second_new: float32 [1, 768, 768], P(None, 'dp')
- up_new: float32 [1, 768, 3072], P(None, 'dp')
- up_first_new: float32 [1, 768, 3072], P(None, 'dp')
- up_second_new: float32 [1, 768, 3072], P(None, 'dp')
- down_new: float32 [1, 3072, 768], P(None, 'dp')
- down_first_new: float32 [1, 3072, 768], P(None, 'dp')
- down_second_new: float32 [1, 3072, 768], P(None, 'dp')
- embed_new: float32 [15360, 768], P(('dp', 'vocab'))
- embed_first_new: float32 [15360, 768], P(('dp', 'vocab'))
- embed_second_new: float32 [15360, 768], P(('dp', 'vocab'))
- vectors_new: float32 [1, 9216], replicated
- vectors_first_new: float32 [1, 9216], replicated
- vectors_second_new: float32 [1, 9216], replicated
- extras_new: float32 [406, 768], replicated
- extras_first_new: float32 [406, 768], replicated
- extras_second_new: float32 [406, 768], replicated
All inputs are finite; a program needn't handle non-finite values. No bound on the sum of `resets` on one device may be relied on, other than what follows from the above.
Results may differ from a plain program's by a relative error of at most 0.006.
Values may be sent and summed in bfloat16 or wider, within the bound.
A program may use at most 256 MiB of HBM per device.

v0:
```python
import jax
import jax.numpy as jnp
from jax import lax
from jax.sharding import PartitionSpec as P

D = 768
HEADS = 12
HD = 64
FF = 3072
MEM = 10
SEG = 364
SEGS = 2
LAYERS = 1
MLM = 112
ROWS = 384


BETA_ONE = 0.9
BETA_TWO = 0.999
ADAM_EPS = 1e-08
DECAY = 0.01
LN_EPS = 1e-06
CLIP = 0.02
LR_BIG = 0.04
LR_SMALL = 0.5
MASKED = -1000000000.0


def layer_norm(values, gain, shift):
    mean = jnp.mean(values, axis=-1, keepdims=True)
    centered = values - mean
    var = jnp.mean(centered * centered, axis=-1, keepdims=True)
    return centered * lax.rsqrt(var + LN_EPS) * gain + shift


def gelu_exact(values):
    return jax.nn.gelu(values, approximate=False)


def split_vec(vec):
    widths = [D, D, D, D, D, FF, D, D, D]
    parts = []
    start = 0
    for width in widths:
        parts.append(vec[start : start + width])
        start += width
    return parts


def mask_of(doc_row):
    marks = jnp.full((MEM,), -1, jnp.int32)
    full = jnp.concatenate([marks, doc_row, marks])
    memory = full < 0
    return (full[:, None] == full[None, :]) | memory[:, None] | memory[None, :]


def contract(left, right):
    return jnp.einsum("rk,rn->kn", left, right, preferred_element_type=jnp.float32)


def back_through(grad, weight):
    return jnp.einsum("rn,kn->rk", grad, weight, preferred_element_type=jnp.float32)


def col_sum(values):
    return jnp.sum(values.astype(jnp.float32), axis=0)


def squares(arrays):
    total = jnp.zeros((), jnp.float32)
    for values in arrays:
        total = total + jnp.sum(values * values)
    return total


def split_heads(proj):
    rows = proj.shape[0]
    return [proj[:, k * D : (k + 1) * D].reshape(rows, HEADS, HD) for k in range(3)]


def attend(proj, allowed):
    query, keyed, values = split_heads(proj)
    scores = jnp.einsum("qhd,khd->hqk", query, keyed, preferred_element_type=jnp.float32) * HD ** (
        -0.5
    )
    scores = jnp.where(allowed[None], scores, MASKED)
    top = jnp.max(scores, axis=-1, keepdims=True)
    expd = jnp.exp(scores - top)
    total = jnp.sum(expd, axis=-1, keepdims=True)
    probs = (expd / total).astype(jnp.bfloat16)
    context = jnp.einsum("hqk,khd->qhd", probs, values, preferred_element_type=jnp.float32)
    return (context.reshape(proj.shape[0], D).astype(jnp.bfloat16), top + jnp.log(total))


def attend_back(proj, allowed, lse, d_context):
    query, keyed, values = split_heads(proj)
    rows = proj.shape[0]
    scale = HD ** (-0.5)
    scores = jnp.einsum("qhd,khd->hqk", query, keyed, preferred_element_type=jnp.float32) * scale
    probs = jnp.exp(jnp.where(allowed[None], scores, MASKED) - lse)
    d_ctx = d_context.reshape(rows, HEADS, HD)
    d_probs = jnp.einsum("qhd,khd->hqk", d_ctx, values, preferred_element_type=jnp.float32)
    d_values = jnp.einsum(
        "hqk,qhd->khd", probs.astype(jnp.bfloat16), d_ctx, preferred_element_type=jnp.float32
    )
    d_scores = (probs * (d_probs - jnp.sum(probs * d_probs, axis=-1, keepdims=True))).astype(
        jnp.bfloat16
    )
    d_query = (
        jnp.einsum("hqk,khd->qhd", d_scores, keyed, preferred_element_type=jnp.float32) * scale
    )
    d_keyed = (
        jnp.einsum("hqk,qhd->khd", d_scores, query, preferred_element_type=jnp.float32) * scale
    )
    return jnp.concatenate(
        [d_query.reshape(rows, D), d_keyed.reshape(rows, D), d_values.reshape(rows, D)], axis=1
    )


def layer_forward(hidden, weights, vec, allowed):
    w_qkv, w_out, w_up, w_down = weights
    b_q, b_v, b_o, g_one, b_one, b_up, b_down, g_two, b_two = split_vec(vec)
    hidden_low = hidden.astype(jnp.bfloat16)
    bias = jnp.concatenate([b_q, jnp.zeros_like(b_q), b_v])
    proj = (jnp.dot(hidden_low, w_qkv, preferred_element_type=jnp.float32) + bias).astype(
        jnp.bfloat16
    )
    context, lse = attend(proj, allowed)
    sum_one = hidden + (jnp.dot(context, w_out, preferred_element_type=jnp.float32) + b_o)
    mid = layer_norm(sum_one, g_one, b_one)
    mid_low = mid.astype(jnp.bfloat16)
    upped = jnp.dot(mid_low, w_up, preferred_element_type=jnp.float32) + b_up
    act = gelu_exact(upped).astype(jnp.bfloat16)
    sum_two = mid + (jnp.dot(act, w_down, preferred_element_type=jnp.float32) + b_down)
    kept = (hidden_low, proj, lse, context, sum_one, mid_low, upped, act, sum_two)
    return (layer_norm(sum_two, g_two, b_two), kept)


def layer_backward(kept, d_out, weights, vec, allowed):
    hidden_low, proj, lse, context, sum_one, mid_low, upped, act, sum_two = kept
    w_qkv, w_out, w_up, w_down = weights
    parts = split_vec(vec)
    norm_two = jax.vjp(layer_norm, sum_two, parts[7], parts[8])[1]
    d_sum_two, d_g_two, d_b_two = norm_two(d_out)
    r_down = d_sum_two.astype(jnp.bfloat16)
    d_w_down = contract(act, r_down)
    gelu_grad = jax.vjp(gelu_exact, upped)[1]
    r_up = gelu_grad(back_through(r_down, w_down))[0].astype(jnp.bfloat16)
    d_w_up = contract(mid_low, r_up)
    d_mid = d_sum_two + back_through(r_up, w_up)
    norm_one = jax.vjp(layer_norm, sum_one, parts[3], parts[4])[1]
    d_sum_one, d_g_one, d_b_one = norm_one(d_mid)
    r_att = d_sum_one.astype(jnp.bfloat16)
    d_w_out = contract(context, r_att)
    d_context = back_through(r_att, w_out).astype(jnp.bfloat16)
    r_proj = attend_back(proj, allowed, lse, d_context).astype(jnp.bfloat16)
    d_w_qkv = contract(hidden_low, r_proj)
    d_hidden = d_sum_one + back_through(r_proj, w_qkv)
    proj_sums = col_sum(r_proj)
    d_vec = jnp.concatenate(
        [
            proj_sums[:D],
            proj_sums[2 * D :],
            col_sum(r_att),
            d_g_one,
            d_b_one,
            col_sum(r_up),
            col_sum(r_down),
            d_g_two,
            d_b_two,
        ]
    )
    return (d_hidden, (d_w_qkv, d_w_out, d_w_up, d_w_down), d_vec)


def adam(master, first, second, grad, coef, count, rate):
    clipped = grad * coef
    first_new = BETA_ONE * first + (1.0 - BETA_ONE) * clipped
    second_new = BETA_TWO * second + (1.0 - BETA_TWO) * clipped * clipped
    first_hat = first_new / (1.0 - BETA_ONE**count)
    second_hat = second_new / (1.0 - BETA_TWO**count)
    master_new = master - rate * (first_hat / (jnp.sqrt(second_hat) + ADAM_EPS) + DECAY * master)
    return (master_new, first_new, second_new)


def per_device(
    ids,
    docs,
    resets,
    mlm_pos,
    mlm_label,
    step,
    qkv_master,
    qkv_first,
    qkv_second,
    out_master,
    out_first,
    out_second,
    up_master,
    up_first,
    up_second,
    down_master,
    down_first,
    down_second,
    embed_master,
    embed_first,
    embed_second,
    vectors_master,
    vectors_first,
    vectors_second,
    extras_master,
    extras_first,
    extras_second,
):
    w_qkv, w_out, w_up, w_down, table = (
        lax.all_gather(qkv_master.astype(jnp.bfloat16), "dp", axis=1, tiled=True),
        lax.all_gather(out_master.astype(jnp.bfloat16), "dp", axis=1, tiled=True),
        lax.all_gather(up_master.astype(jnp.bfloat16), "dp", axis=1, tiled=True),
        lax.all_gather(down_master.astype(jnp.bfloat16), "dp", axis=1, tiled=True),
        lax.all_gather(embed_master.astype(jnp.bfloat16), "dp", axis=0, tiled=True),
    )
    n_dp = lax.axis_size("dp")
    n_vocab = lax.axis_size("vocab")
    dp_idx = lax.axis_index("dp")
    vocab_idx = lax.axis_index("vocab")
    count = ids.shape[0] * n_dp * MLM
    per = table.shape[0] // n_dp
    slots = jnp.arange(table.shape[0], dtype=jnp.int32)
    row_ids = (slots // per * n_vocab + vocab_idx) * per + slots % per
    pos_rows = extras_master[:ROWS]
    first_mem = extras_master[ROWS : ROWS + MEM]
    write_mem = extras_master[ROWS + MEM : ROWS + 2 * MEM]
    gain_e = extras_master[ROWS + 2 * MEM]
    bias_e = extras_master[ROWS + 2 * MEM + 1]

    def layer_weights(lay):
        return (w_qkv[lay], w_out[lay], w_up[lay], w_down[lay])

    def run_item(carry, item):
        ids_row, doc_row, reset_row, positions, labels = item
        loss_now, g_qkv, g_out, g_up, g_down, g_table, g_vec, g_ext = carry
        onehot = (ids_row[:, None] == row_ids[None, :]).astype(jnp.bfloat16)
        tokens = lax.psum(
            jnp.dot(onehot, table, preferred_element_type=jnp.float32).astype(jnp.bfloat16), "vocab"
        ).astype(jnp.float32)
        memory = first_mem
        saves = []
        finals = []
        for seg in range(SEGS):
            if seg > 0:
                memory = jnp.where(reset_row[seg - 1] > 0, first_mem, memory)
            allowed = mask_of(doc_row[seg * SEG : (seg + 1) * SEG])
            start_x = (
                jnp.concatenate([memory, tokens[seg * SEG : (seg + 1) * SEG], write_mem]) + pos_rows
            )
            hidden = layer_norm(start_x, gain_e, bias_e)
            kept_layers = []
            lay = 0
            hidden, kept = layer_forward(hidden, layer_weights(lay), vectors_master[lay], allowed)
            kept_layers.append(kept)
            saves.append((start_x, allowed, kept_layers))
            memory = hidden[MEM + SEG :]
            finals.append(hidden[MEM : MEM + SEG])
        chosen = jnp.concatenate(finals)[positions].astype(jnp.bfloat16)
        logits = jnp.einsum("md,vd->mv", chosen, table, preferred_element_type=jnp.float32)
        hits = labels[:, None] == row_ids[None, :]
        target_part = jnp.sum(jnp.where(hits, logits, 0.0), axis=-1)
        top = lax.pmax(jnp.max(logits, axis=-1), "vocab")
        sums, target = lax.psum(
            (jnp.sum(jnp.exp(logits - top[:, None]), axis=-1), target_part), "vocab"
        )
        lse = top + jnp.log(sums)
        item_loss = jnp.sum(lse - target) / count
        d_logits = ((jnp.exp(logits - lse[:, None]) - hits.astype(jnp.float32)) / count).astype(
            jnp.bfloat16
        )
        d_table = jnp.einsum("mv,md->vd", d_logits, chosen, preferred_element_type=jnp.float32)
        d_chosen = lax.psum(
            jnp.einsum("mv,vd->md", d_logits, table, preferred_element_type=jnp.float32), "vocab"
        )
        d_final = jnp.zeros((SEGS * SEG, D), jnp.float32).at[positions].add(d_chosen)
        layer_acc = [g_qkv, g_out, g_up, g_down]
        d_memory = jnp.zeros((MEM, D), jnp.float32)
        d_pos = jnp.zeros((ROWS, D), jnp.float32)
        d_first = jnp.zeros((MEM, D), jnp.float32)
        d_write = jnp.zeros((MEM, D), jnp.float32)
        d_gain = jnp.zeros((D,), jnp.float32)
        d_bias = jnp.zeros((D,), jnp.float32)
        d_tokens = [None] * SEGS
        for seg in reversed(range(SEGS)):
            start_x, allowed, kept_layers = saves[seg]
            d_hidden = jnp.concatenate(
                [jnp.zeros((MEM, D), jnp.float32), d_final[seg * SEG : (seg + 1) * SEG], d_memory]
            )
            for lay in reversed(range(LAYERS)):
                d_hidden, d_weights, d_vec = layer_backward(
                    kept_layers[lay], d_hidden, layer_weights(lay), vectors_master[lay], allowed
                )
                layer_acc = [acc.at[lay].add(grad) for acc, grad in zip(layer_acc, d_weights)]
                g_vec = g_vec.at[lay].add(d_vec)
            norm_embed = jax.vjp(layer_norm, start_x, gain_e, bias_e)[1]
            d_x, d_g, d_b = norm_embed(d_hidden)
            d_pos = d_pos + d_x
            d_gain = d_gain + d_g
            d_bias = d_bias + d_b
            d_write = d_write + d_x[MEM + SEG :]
            d_tokens[seg] = d_x[MEM : MEM + SEG]
            d_read = d_x[:MEM]
            if seg > 0:
                resetting = reset_row[seg - 1] > 0
                d_first = d_first + jnp.where(resetting, d_read, 0.0)
                d_memory = jnp.where(resetting, 0.0, d_read)
            else:
                d_first = d_first + d_read
        d_tok = jnp.concatenate(d_tokens).astype(jnp.bfloat16)
        d_table = d_table + jnp.einsum(
            "tv,td->vd", onehot, d_tok, preferred_element_type=jnp.float32
        )
        d_ext = jnp.concatenate([d_pos, d_first, d_write, d_gain[None], d_bias[None]])
        out_carry = (
            loss_now + item_loss,
            layer_acc[0],
            layer_acc[1],
            layer_acc[2],
            layer_acc[3],
            g_table + d_table,
            g_vec,
            g_ext + d_ext,
        )
        return (out_carry, None)

    zero_carry = (
        jnp.zeros((), jnp.float32),
        jnp.zeros(w_qkv.shape, jnp.float32),
        jnp.zeros(w_out.shape, jnp.float32),
        jnp.zeros(w_up.shape, jnp.float32),
        jnp.zeros(w_down.shape, jnp.float32),
        jnp.zeros(table.shape, jnp.float32),
        jnp.zeros(vectors_master.shape, jnp.float32),
        jnp.zeros(extras_master.shape, jnp.float32),
    )
    result, _ = lax.scan(run_item, zero_carry, (ids, docs, resets, mlm_pos, mlm_label))
    loss_part, g_qkv, g_out, g_up, g_down, g_table, g_vec, g_ext = result
    loss, g_vec, g_ext = lax.psum((loss_part, g_vec, g_ext), "dp")
    states = (
        (qkv_master, qkv_first, qkv_second),
        (out_master, out_first, out_second),
        (up_master, up_first, up_second),
        (down_master, down_first, down_second),
    )
    s_qkv, s_out, s_up, s_down, s_table = (
        lax.psum_scatter(g_qkv, "dp", scatter_dimension=1, tiled=True),
        lax.psum_scatter(g_out, "dp", scatter_dimension=1, tiled=True),
        lax.psum_scatter(g_up, "dp", scatter_dimension=1, tiled=True),
        lax.psum_scatter(g_down, "dp", scatter_dimension=1, tiled=True),
        lax.psum_scatter(g_table, "dp", scatter_dimension=0, tiled=True),
    )
    layer_sq = jnp.where(vocab_idx == 0, squares((s_qkv, s_out, s_up, s_down)), 0.0)
    small_sq = jnp.where((vocab_idx == 0) & (dp_idx == 0), squares((g_vec, g_ext)), 0.0)
    norm = jnp.sqrt(lax.psum(layer_sq + squares((s_table,)) + small_sq, ("dp", "vocab")))
    coef = jnp.minimum(1.0, CLIP / (norm + 1e-06))
    step_count = step[0].astype(jnp.float32)
    q_new = adam(states[0][0], states[0][1], states[0][2], s_qkv, coef, step_count, LR_BIG)
    o_new = adam(states[1][0], states[1][1], states[1][2], s_out, coef, step_count, LR_BIG)
    u_new = adam(states[2][0], states[2][1], states[2][2], s_up, coef, step_count, LR_BIG)
    d_new = adam(states[3][0], states[3][1], states[3][2], s_down, coef, step_count, LR_BIG)
    q_out, o_out, u_out, d_out = (q_new, o_new, u_new, d_new)
    e_new = adam(embed_master, embed_first, embed_second, s_table, coef, step_count, LR_BIG)
    v_new = adam(vectors_master, vectors_first, vectors_second, g_vec, coef, step_count, LR_SMALL)
    x_new = adam(extras_master, extras_first, extras_second, g_ext, coef, step_count, LR_SMALL)
    return (
        loss,
        norm,
        q_out[0],
        q_out[1],
        q_out[2],
        o_out[0],
        o_out[1],
        o_out[2],
        u_out[0],
        u_out[1],
        u_out[2],
        d_out[0],
        d_out[1],
        d_out[2],
        e_new[0],
        e_new[1],
        e_new[2],
        v_new[0],
        v_new[1],
        v_new[2],
        x_new[0],
        x_new[1],
        x_new[2],
    )


def solution(mesh):
    in_specs = (
        P("dp", None),
        P("dp", None),
        P("dp", None),
        P("dp", None),
        P("dp", None),
        P(),
        P(None, "dp", None),
        P(None, "dp", None),
        P(None, "dp", None),
        P(None, "dp", None),
        P(None, "dp", None),
        P(None, "dp", None),
        P(None, "dp", None),
        P(None, "dp", None),
        P(None, "dp", None),
        P(None, "dp", None),
        P(None, "dp", None),
        P(None, "dp", None),
        P(("dp", "vocab"), None),
        P(("dp", "vocab"), None),
        P(("dp", "vocab"), None),
        P(),
        P(),
        P(),
        P(),
        P(),
        P(),
    )
    out_specs = (
        P(),
        P(),
        P(None, "dp", None),
        P(None, "dp", None),
        P(None, "dp", None),
        P(None, "dp", None),
        P(None, "dp", None),
        P(None, "dp", None),
        P(None, "dp", None),
        P(None, "dp", None),
        P(None, "dp", None),
        P(None, "dp", None),
        P(None, "dp", None),
        P(None, "dp", None),
        P(("dp", "vocab"), None),
        P(("dp", "vocab"), None),
        P(("dp", "vocab"), None),
        P(),
        P(),
        P(),
        P(),
        P(),
        P(),
    )
    return jax.shard_map(
        per_device, mesh=mesh, in_specs=in_specs, out_specs=out_specs, check_vma=False
    )
```

profile of v0, /device:TPU:0, one launch (start us, length us, event | category | flops | bytes accessed | tf_op | source)
XLA Modules:
  0.0 1514.4 jit_solution(14740966620096690262)
XLA Ops:
  9.7 98.0 %all-gather.6.cloned.1.call-done = bf16[3840,768]{1,0:T(8,128)(2,1)} async-done(((bf16[480,768]{1,0:T(8,128)(2,1)}), bf16[3840,768]{1,0:T(8,128)(2,1)}) %all-gather.6.cloned.1.call-update) | async-done | bytes 5898256 | tf_op jit(solution)/shard_map/all_gather | solution.py:220
  107.8 8.2 fusion.70
  125.2 26.0 %all-reduce.6.cloned.1.call-done = bf16[728,768]{1,0:T(8,128)(2,1)} async-done(((bf16[728,768]{1,0:T(8,128)(2,1)}), bf16[728,768]{1,0:T(8,128)(2,1)}) %all-reduce.6.cloned.1.call-update) | async-done | bytes 1118224 | tf_op jit(solution)/shard_map/while/body/eval_jaxpr/psum | solution.py:243
  154.2 65.3 %all-gather.8.cloned.1.call-done = bf16[1,768,2304]{2,1,0:T(8,128)(2,1)} async-done(((bf16[1,96,2304]{2,1,0:T(8,128)(2,1)}), bf16[1,768,2304]{2,1,0:T(8,128)(2,1)}) %all-gather.8.cloned.1.call-update) | async-done | bytes 3538960 | tf_op jit(solution)/shard_map/all_gather | solution.py:216
  231.0 30.7 %all-gather.10.cloned.1.call-done = bf16[1,768,768]{2,1,0:T(8,128)(2,1)} async-done(((bf16[1,96,768]{2,1,0:T(8,128)(2,1)}), bf16[1,768,768]{2,1,0:T(8,128)(2,1)}) %all-gather.10.cloned.1.call-update) | async-done | bytes 1179664 | tf_op jit(solution)/shard_map/all_gather | solution.py:217
  264.2 78.8 %all-gather.12.cloned.1.call-done = bf16[1,768,3072]{2,1,0:T(8,128)(2,1)} async-done(((bf16[1,96,3072]{2,1,0:T(8,128)(2,1)}), bf16[1,768,3072]{2,1,0:T(8,128)(2,1)}) %all-gather.12.cloned.1.call-update) | async-done | bytes 4718608 | tf_op jit(solution)/shard_map/all_gather | solution.py:218
  343.0 15.6 %multiply_convert_fusion.3 = (bf16[384,3072]{1,0:T(8,128)(2,1)}, f32[384,3072]{1,0:T(8,128)}, f32[384,3072]{1,0:T(8,128)}) fusion(f32[3072]{0:T(1024)S(1)} %bitcast.224, bf16[1,768,3072]{2,1,0:T(8,128)(2,1)} %all-gather.12.cloned.1.call-done, f32[384,768]{1,0:T(8,128)S(1)} %get-tuple-element.387, f32[768]{0:T(1024)S(1)} %get-tuple-element.295, ...), kind=kOutput, calls=%fused_computation.67 | convolution fusion | flops 1891270656 | bytes 17716224 | tf_op jit(solution)/shard_map/while/body/eval_jaxpr/dot_general | solution.py:132
  358.7 65.0 %all-gather.14.cloned.1.call-done = bf16[1,3072,768]{2,1,0:T(8,128)(2,1)} async-done(((bf16[1,384,768]{2,1,0:T(8,128)(2,1)}), bf16[1,3072,768]{2,1,0:T(8,128)(2,1)}) %all-gather.14.cloned.1.call-update) | async-done | bytes 4718608 | tf_op jit(solution)/shard_map/all_gather | solution.py:219
  448.2 16.1 %multiply_convert_fusion.2 = (bf16[384,3072]{1,0:T(8,128)(2,1)S(1)}, f32[384,3072]{1,0:T(8,128)}, f32[384,3072]{1,0:T(8,128)}) fusion(f32[3072]{0:T(1024)S(1)} %bitcast.225, bf16[1,768,3072]{2,1,0:T(8,128)(2,1)} %all-gather.12.cloned.1.call-done, f32[384,768]{1,0:T(8,128)S(1)} %get-tuple-element.394, f32[384]{0:T(512)S(1)} %fusion.154, ...), kind=kOutput, calls=%fused_computation.54 | convolution fusion | flops 1891270656 | bytes 17716224 | tf_op jit(solution)/shard_map/while/body/eval_jaxpr/dot_general | solution.py:132
  480.9 6.6 all-reduce.1
  492.8 30.0 %all-reduce.8.cloned.1.call-done = f32[112,768]{1,0:T(8,128)} async-done(((f32[112,768]{1,0:T(8,128)}), f32[112,768]{1,0:T(8,128)}) %all-reduce.8.cloned.1.call-update) | async-done | bytes 344080 | tf_op jit(solution)/shard_map/while/body/eval_jaxpr/psum | solution.py:278
  532.0 8.3 convert_reduce_fusion.1
  548.4 8.2 multiply_reduce_fusion.1
  575.7 8.6 convert_reduce_fusion
  592.3 7.5 multiply_reduce_fusion
  618.5 7.3 concatenate.183
  671.2 6.4 convolution_add_fusion
  681.7 38.6 %all-reduce = (f32[]{:T(128)}, f32[1,9216]{1,0:T(1,128)S(1)}) all-reduce(f32[]{:T(128)S(6)} %div.303, f32[1,9216]{1,0:T(1,128)S(1)} %add.682), channel_id=1, replica_groups=mesh['dp'=8,'vocab'=4] {'dp'}, use_global_device_ids=true, to_apply=%region_24.25 | all-reduce | flops 9217 | bytes 73736 | tf_op jit(solution)/shard_map/psum | solution.py:344
  724.5 56.5 %reduce-scatter.8.cloned.1.call-done = f32[1,96,768]{2,1,0:T(8,128)} async-done(((f32[1,768,768]{2,1,0:T(8,128)}), f32[1,96,768]{2,1,0:T(8,128)}) %reduce-scatter.8.cloned.1.call-update) | async-done | bytes 294928 | tf_op jit(solution)/shard_map/reduce_scatter | solution.py:353
  782.6 130.5 %reduce-scatter.6.cloned.1.call-done = f32[1,96,2304]{2,1,0:T(8,128)} async-done(((f32[1,768,2304]{2,1,0:T(8,128)}), f32[1,96,2304]{2,1,0:T(8,128)}) %reduce-scatter.6.cloned.1.call-update) | async-done | bytes 884752 | tf_op jit(solution)/shard_map/reduce_scatter | solution.py:352
  916.3 162.7 %reduce-scatter.10.cloned.1.call-done = f32[1,96,3072]{2,1,0:T(8,128)} async-done(((f32[1,768,3072]{2,1,0:T(8,128)}), f32[1,96,3072]{2,1,0:T(8,128)}) %reduce-scatter.10.cloned.1.call-update) | async-done | bytes 1179664 | tf_op jit(solution)/shard_map/reduce_scatter | solution.py:354
  1082.0 162.9 %reduce-scatter.12.cloned.1.call-done = f32[1,384,768]{2,1,0:T(8,128)} async-done(((f32[1,3072,768]{2,1,0:T(8,128)}), f32[1,384,768]{2,1,0:T(8,128)}) %reduce-scatter.12.cloned.1.call-update) | async-done | bytes 1179664 | tf_op jit(solution)/shard_map/reduce_scatter | solution.py:355
  1247.8 196.3 %reduce-scatter.14.cloned.1.call-done = f32[480,768]{1,0:T(8,128)} async-done(((f32[3840,768]{1,0:T(8,128)}), f32[480,768]{1,0:T(8,128)}) %reduce-scatter.14.cloned.1.call-update) | async-done | bytes 1474576 | tf_op jit(solution)/shard_map/reduce_scatter | solution.py:356
  1447.0 39.6 %psum.67 = f32[]{:T(128)} all-reduce(f32[]{:T(128)S(6)} %add.691), channel_id=1, replica_groups=mesh['dp'=8,'vocab'=4] {'dp','vocab'}, use_global_device_ids=true, to_apply=%region_76.77 | all-reduce | flops 1 | bytes 8 | tf_op jit(solution)/shard_map/psum | solution.py:360
  (596 shorter events, 215.5 us)
Async XLA Ops:
  7.2 100.6 %all-gather.6.cloned.1.call-start = ((), (), s32[]{:S(2)}) async-start(), calls=%async_computation.5 | async-start | bytes 6635520 | tf_op jit(solution)/shard_map/all_gather | solution.py:220
  9.6 141.6 %all-reduce.6.cloned.1.call-start = ((), (), s32[]{:S(2)}) async-start(), calls=%async_computation.6 | async-start | bytes 2236416 | tf_op jit(solution)/shard_map/while/body/eval_jaxpr/psum | solution.py:243
  9.7 98.1 %copy-start.170 = (s32[728]{0:T(1024)}, s32[728]{0:T(1024)S(1)}, u32[]{:S(2)}) copy-start(s32[728]{0:T(1024)S(1)} %reduce.36) | copy-start | bytes 8740
  9.7 98.1 %copy-start.94 = (s32[3840]{0:T(1024)}, s32[3840]{0:T(1024)S(1)}, u32[]{:S(2)}) copy-start(s32[3840]{0:T(1024)S(1)} %fusion.148) | copy-start | bytes 46084
  116.0 103.5 %all-gather.8.cloned.1.call-start = ((), (), s32[]{:S(2)}) async-start(), calls=%async_computation.7 | async-start | bytes 3981312 | tf_op jit(solution)/shard_map/all_gather | solution.py:216
  118.0 143.7 %all-gather.10.cloned.1.call-start = ((), (), s32[]{:S(2)}) async-start(), calls=%async_computation.8 | async-start | bytes 1327104 | tf_op jit(solution)/shard_map/all_gather | solution.py:217
  118.8 224.3 %all-gather.12.cloned.1.call-start = ((), (), s32[]{:S(2)}) async-start(), calls=%async_computation.9 | async-start | bytes 5308416 | tf_op jit(solution)/shard_map/all_gather | solution.py:218
  119.7 303.9 %all-gather.14.cloned.1.call-start = ((), (), s32[]{:S(2)}) async-start(), calls=%async_computation.10 | async-start | bytes 5308416 | tf_op jit(solution)/shard_map/all_gather | solution.py:219
  120.7 402.0 %all-reduce.8.cloned.1.call-start = ((), (), s32[]{:S(2)}) async-start(), calls=%async_computation.11 | async-start | bytes 688128 | tf_op jit(solution)/shard_map/while/body/eval_jaxpr/psum | solution.py:278
  153.9 107.8 %copy-start.2 = (f32[384,768]{1,0:T(8,128)}, f32[384,768]{1,0:T(8,128)S(1)}, u32[]{:S(2)}) copy-start(f32[384,768]{1,0:T(8,128)S(1)} %get-tuple-element.361) | copy-start | bytes 3538948
  263.9 159.8 %copy-start.11 = (f32[384,768]{1,0:T(8,128)}, f32[384,768]{1,0:T(8,128)S(1)}, u32[]{:S(2)}) copy-start(f32[384,768]{1,0:T(8,128)S(1)} %get-tuple-element.387) | copy-start | bytes 3538948
  263.9 159.8 %copy-start.105 = (f32[384]{0:T(512)}, f32[384]{0:T(512)S(1)}, u32[]{:S(2)}) copy-start(f32[384]{0:T(512)S(1)} %broadcast_multiply_fusion.4) | copy-start | bytes 4612
  264.2 159.5 %copy-start.121 = (f32[384]{0:T(512)}, f32[384]{0:T(512)S(1)}, u32[]{:S(2)}) copy-start(f32[384]{0:T(512)S(1)} %fusion.151) | copy-start | bytes 4612
  492.7 228.2 %all-reduce.10.cloned.1.call-start = ((), (), s32[]{:S(2)}) async-start(), calls=%async_computation.17 | async-start | bytes 2506752 | tf_op jit(solution)/shard_map/psum | solution.py:344
  625.8 155.1 %reduce-scatter.8.cloned.1.call-start = ((), (), s32[]{:S(2)}) async-start(), calls=%async_computation.13 | async-start | bytes 2654208 | tf_op jit(solution)/shard_map/reduce_scatter | solution.py:353
  630.6 282.5 %reduce-scatter.6.cloned.1.call-start = ((), (), s32[]{:S(2)}) async-start(), calls=%async_computation.12 | async-start | bytes 7962624 | tf_op jit(solution)/shard_map/reduce_scatter | solution.py:352
  640.8 438.2 %reduce-scatter.10.cloned.1.call-start = ((), (), s32[]{:S(2)}) async-start(), calls=%async_computation.14 | async-start | bytes 10616832 | tf_op jit(solution)/shard_map/reduce_scatter | solution.py:354
  652.1 592.8 %reduce-scatter.12.cloned.1.call-start = ((), (), s32[]{:S(2)}) async-start(), calls=%async_computation.15 | async-start | bytes 10616832 | tf_op jit(solution)/shard_map/reduce_scatter | solution.py:355
  662.3 781.8 %reduce-scatter.14.cloned.1.call-start = ((), (), s32[]{:S(2)}) async-start(), calls=%async_computation.16 | async-start | bytes 13271040 | tf_op jit(solution)/shard_map/reduce_scatter | solution.py:356
  1081.2 406.1 %copy-start.100 = (f32[1,9216]{1,0:T(1,128)S(1)}, f32[1,9216]{1,0:T(1,128)}, u32[]{:S(2)}) copy-start(f32[1,9216]{1,0:T(1,128)} %param.68) | copy-start | bytes 110596
  1081.2 406.2 %copy-start.115 = (f32[1,9216]{1,0:T(1,128)S(1)}, f32[1,9216]{1,0:T(1,128)}, u32[]{:S(2)}) copy-start(f32[1,9216]{1,0:T(1,128)} %param.70) | copy-start | bytes 110596
  1081.2 406.2 %copy-start.116 = (f32[1,9216]{1,0:T(1,128)S(1)}, f32[1,9216]{1,0:T(1,128)}, u32[]{:S(2)}) copy-start(f32[1,9216]{1,0:T(1,128)} %param.69) | copy-start | bytes 110596
  1081.2 407.1 %copy-start.16 = (f32[406,768]{1,0:T(8,128)S(1)}, f32[406,768]{1,0:T(8,128)}, u32[]{:S(2)}) copy-start(f32[406,768]{1,0:T(8,128)} %param.71) | copy-start | bytes 3741700
  1081.2 407.1 %copy-start.43 = (f32[406,768]{1,0:T(8,128)S(1)}, f32[406,768]{1,0:T(8,128)}, u32[]{:S(2)}) copy-start(f32[406,768]{1,0:T(8,128)} %all-reduce.10.cloned.1.call-done) | copy-start | bytes 3741700
  (183 other events, 1289.8 us)
Sparse Core Ops, SparseCore 0:
  10.8 96.9 all-gather.5
  116.1 35.0 all-reduce.5
  154.0 65.5 all-gather.7
  222.1 39.5 all-gather.9
  264.3 78.6 all-gather.11
  345.6 78.0 all-gather.13
  492.8 29.8 all-reduce.7
  625.9 82.7 all-reduce.9
  712.6 68.2 reduce-scatter.7
  784.9 128.0 reduce-scatter.5
  916.6 162.3 reduce-scatter.9
  1082.5 162.3 reduce-scatter.11
  1248.5 195.4 reduce-scatter.13
where the time goes:
time: 1520 us; the launch traced here: 1510 us
  waiting for transfers between devices  1100 us (72%)
  matrix products  177 us (12%)
  blocking collectives  90.4 us (6%)
  other arithmetic  71.4 us (5%)
  local copies, waits for them, and re-layouts  46.1 us (3%)
  between operations  25.3 us (2%)
    reduce_scatter x1, waiting for transfers between devices, per_device(): lax.psum_scatter(g_table, 'dp', scatter_dimension=0, tiled=True)  196 us
    reduce_scatter x1, waiting for transfers between devices, per_device(): lax.psum_scatter(g_down, 'dp', scatter_dimension=1, tiled=True)  163 us
    reduce_scatter x1, waiting for transfers between devices, per_device(): lax.psum_scatter(g_up, 'dp', scatter_dimension=1, tiled=True)  163 us
    reduce_scatter x1, waiting for transfers between devices, per_device(): lax.psum_scatter(g_qkv, 'dp', scatter_dimension=1, tiled=True)  130 us
    all_gather x1, waiting for transfers between devices, per_device(): lax.all_gather(embed_master.astype(jnp.bfloat16), 'dp', axis=0, tiled=True)  98 us
    all_gather x1, waiting for transfers between devices, per_device(): lax.all_gather(up_master.astype(jnp.bfloat16), 'dp', axis=1, tiled=True)  78.8 us
    all_gather x1, waiting for transfers between devices, per_device(): lax.all_gather(qkv_master.astype(jnp.bfloat16), 'dp', axis=1, tiled=True)  65.3 us
    all_gather x1, waiting for transfers between devices, per_device(): lax.all_gather(down_master.astype(jnp.bfloat16), 'dp', axis=1, tiled=True)  65 us
  transfers between devices with their start and end apart: 13, of which 12 were waited for; matrix products, arithmetic and copies ran while one was open for 7% of the time, Pallas kernels for 0%

commit v1 on v0

v1 whole, which is shorter than its diff:
```python
import functools

import jax
import jax.numpy as jnp
from jax import lax
from jax.experimental import pallas as pl
from jax.experimental.pallas import tpu as pltpu
from jax.sharding import PartitionSpec as P

D = 768
HEADS = 12
HD = 64
FF = 3072
MEM = 10
SEG = 364
SEGS = 2
LAYERS = 1
MLM = 112
ROWS = 384


BETA_ONE = 0.9
BETA_TWO = 0.999
ADAM_EPS = 1e-08
DECAY = 0.01
LN_EPS = 1e-06
CLIP = 0.02
LR_BIG = 0.04
LR_SMALL = 0.5
MASKED = -1000000000.0


def squares(arrays):
    total = jnp.zeros((), jnp.float32)
    for values in arrays:
        total = total + jnp.sum(values * values)
    return total


def adam(master, first, second, grad, coef, count, rate):
    clipped = grad * coef
    first_new = BETA_ONE * first + (1.0 - BETA_ONE) * clipped
    second_new = BETA_TWO * second + (1.0 - BETA_TWO) * clipped * clipped
    first_hat = first_new / (1.0 - BETA_ONE**count)
    second_hat = second_new / (1.0 - BETA_TWO**count)
    master_new = master - rate * (first_hat / (jnp.sqrt(second_hat) + ADAM_EPS) + DECAY * master)
    return (master_new, first_new, second_new)


MESH = pl.DeviceIdType.MESH
MLM_PAD = 128
EXT = ROWS + 2 * MEM + 2


class Place:
    def __init__(self, n_dp, n_v):
        self.A, self.Y = n_dp // 2, n_v // 2
        self.d, self.v = lax.axis_index("dp"), lax.axis_index("vocab")
        self.a, self.x = self.d // 2, self.d % 2
        self.y, self.c = self.v // 2, self.v % 2
        self.me = (self.d, self.v)
        self.xp = (self.d + 1 - 2 * self.x, self.v)
        self.cp = (self.d, self.v + 1 - 2 * self.c)

    def from_a(self, k):
        return lax.rem(self.a + self.A - k, self.A)

    def to_a(self, k):
        return lax.rem(self.a + k, self.A)

    def from_y(self, k):
        return lax.rem(self.y + self.Y - k, self.Y)

    def zp(self, k):
        return (self.to_a(k) * 2 + self.x, self.v)

    def yp(self, k):
        return (self.d, lax.rem(self.y + k, self.Y) * 2 + self.c)

    def barrier(self, extra=()):
        sem = pltpu.get_barrier_semaphore()
        partners = [self.zp(k) for k in range(1, self.A)] + [self.xp]
        partners += [self.yp(k) for k in range(1, self.Y)] + [self.cp] + list(extra)
        for partner in partners:
            pl.semaphore_signal(sem, 1, device_id=partner, device_id_type=MESH)
        pl.semaphore_wait(sem, len(partners))


class Copies:
    def __init__(self, me, send_sem, recv_sem):
        self.me, self.send_sem, self.recv_sem, self.started = me, send_sem, recv_sem, []

    def send(self, number, src, dst, partner):
        copy = pltpu.make_async_remote_copy(
            src, dst, self.send_sem.at[number], self.recv_sem.at[number], partner, MESH
        )
        copy.start()
        self.started.append(copy)

    def arrived(self, number, dst):
        pltpu.make_async_remote_copy(
            dst, dst, self.send_sem.at[number], self.recv_sem.at[number], self.me, MESH
        ).wait_recv()

    def finish(self):
        for copy in self.started:
            copy.wait_send()


class Gather:
    def __init__(self, place, copies, base, ref, own=None):
        self.p, self.q, self.base, self.ref, self.own = place, copies, base, ref, own
        A, Y = place.A, place.Y
        self.x0 = base + A - 1
        self.y0 = self.x0 + A
        self.c0 = self.y0 + 2 * A * (Y - 1)
        self.end = self.c0 + 2 * A * Y

    @staticmethod
    def count(n_dp, n_v):
        A, Y = n_dp // 2, n_v // 2
        return A - 1 + A + 2 * A * (Y - 1) + 2 * A * Y

    def at(self, slot, j=0, c=None):
        p = self.p
        k = slot % p.A
        x = p.x if slot < p.A else 1 - p.x
        c = p.c if c is None else c
        return self.ref(p.from_a(k) * 2 + x, p.from_y(j) * 2 + c)

    def spread(self, slot):
        p = self.p
        src = self.at(slot) if (slot or self.own is None) else self.own
        if slot < p.A:
            self.q.send(self.x0 + slot, src, self.at(slot), p.xp)
        for k in range(1, p.Y):
            self.q.send(self.y0 + slot * (p.Y - 1) + k - 1, src, self.at(slot), p.yp(k))
        self.q.send(self.c0 + slot * p.Y, src, self.at(slot), p.cp)

    def start(self):
        p = self.p
        src = self.at(0) if self.own is None else self.own
        for k in range(1, p.A):
            self.q.send(self.base + k - 1, src, self.at(0), p.zp(k))
        self.spread(0)

    def step_a(self):
        for k in range(1, self.p.A):
            self.q.arrived(self.base + k - 1, self.at(k))
            self.spread(k)

    def step_x(self):
        A = self.p.A
        for k in range(A):
            self.q.arrived(self.x0 + k, self.at(A + k))
            self.spread(A + k)

    def step_y(self):
        p = self.p
        for slot in range(2 * p.A):
            for j in range(1, p.Y):
                self.q.arrived(self.y0 + slot * (p.Y - 1) + j - 1, self.at(slot, j))
                self.q.send(self.c0 + slot * p.Y + j, self.at(slot, j), self.at(slot, j), p.cp)

    def step_c(self):
        p = self.p
        for slot in range(2 * p.A):
            for j in range(p.Y):
                self.q.arrived(self.c0 + slot * p.Y + j, self.at(slot, j, 1 - p.c))


def weights_kernel(n_dp, n_v, w_ref, tok_ref, out_ref, tok_out, ss, rs, ls):
    p = Place(n_dp, n_v)
    others = []
    for k in range(1, p.A):
        others.append((p.to_a(k) * 2 + 1 - p.x, p.v))
    p.barrier(others)
    q = Copies(p.me, ss, rs)
    groups = w_ref.shape[0] // n_v
    local = pltpu.make_async_copy(tok_ref.at[p.d], tok_out.at[p.d, p.v], ls.at[0])
    local.start()
    locals_ = [local]
    gathers = []
    base = 0
    for g in range(groups):
        own = pltpu.make_async_copy(
            w_ref.at[g * n_v + p.v], out_ref.at[p.d, g * n_v + p.v], ls.at[1 + g]
        )
        own.start()
        locals_.append(own)
        gather = Gather(
            p,
            q,
            base,
            lambda d, v, g=g: out_ref.at[d, g * n_v + v],
            own=w_ref.at[g * n_v + p.v],
        )
        base = gather.end
        gathers.append(gather)
    for k in range(1, n_dp):
        to = lax.rem(p.d + k, n_dp)
        q.send(base + k - 1, tok_ref.at[to], tok_out.at[p.d, p.v], (to, p.v))
    for gather in gathers:
        gather.start()
    local.wait()
    first = base
    base = base + n_dp - 1

    def relay(slot, src_d):
        for k in range(1, p.Y):
            number = base + slot * (p.Y - 1) + k - 1
            q.send(number, tok_out.at[src_d, p.v], tok_out.at[src_d, p.v], p.yp(k))
        number = base + n_dp * (p.Y - 1) + slot * p.Y
        q.send(number, tok_out.at[src_d, p.v], tok_out.at[src_d, p.v], p.cp)

    relay(0, p.d)
    for k in range(1, n_dp):
        src_d = lax.rem(p.d + n_dp - k, n_dp)
        q.arrived(first + k - 1, tok_out.at[src_d, p.v])
        relay(k, src_d)
    for gather in gathers:
        gather.step_a()
    for gather in gathers:
        gather.step_x()
    for slot in range(n_dp):
        src_d = lax.rem(p.d + n_dp - slot, n_dp)
        for j in range(1, p.Y):
            v = p.from_y(j) * 2 + p.c
            q.arrived(base + slot * (p.Y - 1) + j - 1, tok_out.at[src_d, v])
            number = base + n_dp * (p.Y - 1) + slot * p.Y + j
            q.send(number, tok_out.at[src_d, v], tok_out.at[src_d, v], p.cp)
    for gather in gathers:
        gather.step_y()
    for slot in range(n_dp):
        src_d = lax.rem(p.d + n_dp - slot, n_dp)
        for j in range(p.Y):
            v = p.from_y(j) * 2 + 1 - p.c
            q.arrived(base + n_dp * (p.Y - 1) + slot * p.Y + j, tok_out.at[src_d, v])
    for gather in gathers:
        gather.step_c()
    q.finish()
    for copy in locals_[1:]:
        copy.wait()


def gather_weights(blocks, packed, n_dp, n_v):
    groups = blocks.shape[0] // n_v
    count = groups * Gather.count(n_dp, n_v) + (n_dp - 1) + n_dp * (n_v // 2 - 1) + n_dp * (n_v // 2)
    return pl.pallas_call(
        functools.partial(weights_kernel, n_dp, n_v),
        out_shape=(
            jax.ShapeDtypeStruct((n_dp,) + blocks.shape, blocks.dtype),
            jax.ShapeDtypeStruct((n_dp, n_v) + packed.shape[1:], packed.dtype),
        ),
        in_specs=[pl.BlockSpec(memory_space=pl.ANY)] * 2,
        out_specs=(pl.BlockSpec(memory_space=pl.ANY),) * 2,
        scratch_shapes=[
            pltpu.SemaphoreType.DMA((count,)),
            pltpu.SemaphoreType.DMA((count,)),
            pltpu.SemaphoreType.DMA((1 + groups,)),
        ],
        compiler_params=pltpu.CompilerParams(collective_id=0, has_side_effects=True),
    )(blocks, packed)


def chosen_kernel(n_dp, n_v, in_ref, out_ref, ss, rs):
    p = Place(n_dp, n_v)
    p.barrier()
    q = Copies(p.me, ss, rs)
    gather = Gather(p, q, 0, lambda d, v: out_ref.at[d, v])
    out_ref[p.d, p.v] = in_ref[p.v]
    gather.start()
    gather.step_a()
    gather.step_x()
    gather.step_y()
    gather.step_c()
    q.finish()


def gather_chosen(chosen, n_dp, n_v):
    count = Gather.count(n_dp, n_v)
    return pl.pallas_call(
        functools.partial(chosen_kernel, n_dp, n_v),
        out_shape=jax.ShapeDtypeStruct((n_dp,) + chosen.shape, chosen.dtype),
        in_specs=[pl.BlockSpec(memory_space=pltpu.VMEM)],
        out_specs=pl.BlockSpec(memory_space=pltpu.VMEM),
        scratch_shapes=[pltpu.SemaphoreType.DMA((count,)), pltpu.SemaphoreType.DMA((count,))],
        compiler_params=pltpu.CompilerParams(collective_id=1, has_side_effects=True),
    )(chosen)


def d_chosen_kernel(n_dp, n_v, in_ref, out_ref, bc, by, bx, bz, pc, py, px, ss, rs):
    f32, bf = jnp.float32, jnp.bfloat16
    p = Place(n_dp, n_v)
    p.barrier()
    q = Copies(p.me, ss, rs)
    A, Y = p.A, p.Y
    q.send(0, in_ref.at[:, :, :, 1 - p.c], bc, p.cp)
    q.arrived(0, bc)
    pc[...] = (in_ref[:, :, :, p.c].astype(f32) + bc[...].astype(f32)).astype(bf)
    n = 1
    for k in range(1, Y):
        q.send(n + k - 1, pc.at[:, :, lax.rem(p.y + k, Y)], by.at[k - 1], p.yp(k))
    total = pc[:, :, p.y].astype(f32)
    for k in range(1, Y):
        q.arrived(n + k - 1, by.at[k - 1])
        total = total + by[k - 1].astype(f32)
    py[...] = total.astype(bf)
    n = n + Y - 1
    q.send(n, py.at[:, 1 - p.x], bx, p.xp)
    q.arrived(n, bx)
    n = n + 1
    px[...] = (py[:, p.x].astype(f32) + bx[...].astype(f32)).astype(bf)
    for k in range(1, A):
        q.send(n + k - 1, px.at[p.to_a(k)], bz.at[k - 1], p.zp(k))
    total = px[p.a].astype(f32)
    for k in range(1, A):
        q.arrived(n + k - 1, bz.at[k - 1])
        total = total + bz[k - 1].astype(f32)
    n = n + A - 1
    out_ref[p.v] = total.astype(bf)
    for k in range(1, Y):
        q.send(n + k - 1, out_ref.at[p.v], out_ref.at[p.v], p.yp(k))
    q.send(n + Y - 1, out_ref.at[p.v], out_ref.at[p.v], p.cp)
    for j in range(1, Y):
        v = p.from_y(j) * 2 + p.c
        q.arrived(n + j - 1, out_ref.at[v])
        q.send(n + Y - 1 + j, out_ref.at[v], out_ref.at[v], p.cp)
    for j in range(Y):
        v = p.from_y(j) * 2 + 1 - p.c
        q.arrived(n + Y - 1 + j, out_ref.at[v])
    q.finish()


def reduce_d_chosen(partial, n_dp, n_v):
    A, _, Y, _, rows, width = partial.shape
    count = 1 + (Y - 1) + 1 + (A - 1) + (Y - 1) + Y
    kind = partial.dtype
    return pl.pallas_call(
        functools.partial(d_chosen_kernel, n_dp, n_v),
        out_shape=jax.ShapeDtypeStruct((n_v, rows, width), kind),
        in_specs=[pl.BlockSpec(memory_space=pltpu.VMEM)],
        out_specs=pl.BlockSpec(memory_space=pltpu.VMEM),
        scratch_shapes=[
            pltpu.VMEM((A, 2, Y, rows, width), kind),
            pltpu.VMEM((Y - 1, A, 2, rows, width), kind),
            pltpu.VMEM((A, rows, width), kind),
            pltpu.VMEM((A - 1, rows, width), kind),
            pltpu.VMEM((A, 2, Y, rows, width), kind),
            pltpu.VMEM((A, 2, rows, width), kind),
            pltpu.VMEM((A, rows, width), kind),
            pltpu.SemaphoreType.DMA((count,)),
            pltpu.SemaphoreType.DMA((count,)),
        ],
        compiler_params=pltpu.CompilerParams(
            collective_id=2, has_side_effects=True, vmem_limit_bytes=56 << 20
        ),
    )(partial)


def grads_kernel(n_dp, n_v, g_ref, e_ref, t_ref, g_out, e_out, t_out, bx, px, bz, ebx, epx, ebz, ss, rs, ls):
    f32, bf = jnp.float32, jnp.bfloat16
    p = Place(n_dp, n_v)
    A, Y = p.A, p.Y
    p.barrier([(p.to_a(k) * 2 + 1 - p.x, p.v) for k in range(1, A)])
    q = Copies(p.me, ss, rs)
    groups = g_ref.shape[0]
    n = 0
    for g in range(groups):
        q.send(n + g, g_ref.at[g, :, 1 - p.x], bx.at[g], p.xp)
    x0 = n
    n = n + groups
    q.send(n, e_ref.at[:, 1 - p.x], ebx, p.xp)
    ex0 = n
    n = n + 1
    t0 = n
    for k in range(1, n_dp):
        to = lax.rem(p.d + k, n_dp)
        q.send(t0 + k - 1, t_ref.at[to], t_out.at[p.d], (to, p.v))
    n = n + n_dp - 1
    local = pltpu.make_async_copy(t_ref.at[p.d], t_out.at[p.d], ls)
    local.start()
    z0 = n
    n = n + groups * (A - 1)
    ez0 = n
    n = n + A - 1
    for g in range(groups):
        q.arrived(x0 + g, bx.at[g])
        for k in range(1, A + 1):
            to = p.to_a(k)
            px[g, to] = (g_ref[g, to, p.x].astype(f32) + bx[g, to].astype(f32)).astype(bf)
            if k < A:
                q.send(z0 + g * (A - 1) + k - 1, px.at[g, to], bz.at[g, k - 1], p.zp(k))
    q.arrived(ex0, ebx)
    epx[...] = (e_ref[:, p.x].astype(f32) + ebx[...].astype(f32)).astype(bf)
    for k in range(1, A):
        q.send(ez0 + k - 1, epx.at[p.to_a(k)], ebz.at[k - 1], p.zp(k))
    total = epx[p.a].astype(f32)
    for k in range(1, A):
        q.arrived(ez0 + k - 1, ebz.at[k - 1])
        total = total + ebz[k - 1].astype(f32)
    e_out[p.d, p.v] = total.astype(bf)
    small = Gather(p, q, n, lambda d, v: e_out.at[d, v])
    n = small.end
    small.start()
    y0 = n
    n = n + groups * (Y - 1)
    c0 = n
    for g in range(groups):
        total = px[g, p.a].astype(f32)
        for k in range(1, A):
            q.arrived(z0 + g * (A - 1) + k - 1, bz.at[g, k - 1])
            total = total + bz[g, k - 1].astype(f32)
        mine = g_out.at[g * n_v + p.v]
        g_out[g * n_v + p.v] = total.astype(bf)
        for k in range(1, Y):
            q.send(y0 + g * (Y - 1) + k - 1, mine, mine, p.yp(k))
        q.send(c0 + g * Y, mine, mine, p.cp)
    small.step_a()
    small.step_x()
    for g in range(groups):
        for j in range(1, Y):
            piece = g_out.at[g * n_v + p.from_y(j) * 2 + p.c]
            q.arrived(y0 + g * (Y - 1) + j - 1, piece)
            q.send(c0 + g * Y + j, piece, piece, p.cp)
    small.step_y()
    for g in range(groups):
        for j in range(Y):
            q.arrived(c0 + g * Y + j, g_out.at[g * n_v + p.from_y(j) * 2 + 1 - p.c])
    small.step_c()
    for k in range(1, n_dp):
        q.arrived(t0 + k - 1, t_out.at[lax.rem(p.d + n_dp - k, n_dp)])
    q.finish()
    local.wait()


def reduce_grads(grads, extras, tokens, n_dp, n_v):
    A, Y = n_dp // 2, n_v // 2
    groups, _, _, rows, width = grads.shape
    e_rows, e_width = extras.shape[2:]
    kind = grads.dtype
    count = groups * (1 + A - 1 + Y - 1 + Y) + 1 + (n_dp - 1) + (A - 1) + Gather.count(n_dp, n_v)
    vmem = pl.BlockSpec(memory_space=pltpu.VMEM)
    return pl.pallas_call(
        functools.partial(grads_kernel, n_dp, n_v),
        out_shape=(
            jax.ShapeDtypeStruct((groups * n_v, rows, width), kind),
            jax.ShapeDtypeStruct((n_dp, n_v, e_rows, e_width), kind),
            jax.ShapeDtypeStruct(tokens.shape, tokens.dtype),
        ),
        in_specs=[vmem, vmem, vmem],
        out_specs=(vmem, vmem, vmem),
        scratch_shapes=[
            pltpu.VMEM((groups, A, rows, width), kind),
            pltpu.VMEM((groups, A, rows, width), kind),
            pltpu.VMEM((groups, A - 1, rows, width), kind),
            pltpu.VMEM((A, e_rows, e_width), kind),
            pltpu.VMEM((A, e_rows, e_width), kind),
            pltpu.VMEM((A - 1, e_rows, e_width), kind),
            pltpu.SemaphoreType.DMA((count,)),
            pltpu.SemaphoreType.DMA((count,)),
            pltpu.SemaphoreType.DMA,
        ],
        compiler_params=pltpu.CompilerParams(
            collective_id=3, has_side_effects=True, vmem_limit_bytes=56 << 20
        ),
    )(grads, extras, tokens)


def lane_mean(values):
    return jnp.sum(values, axis=-1, keepdims=True) * (1.0 / D)


def norm_parts(values):
    centered = values - lane_mean(values)
    rate = lax.rsqrt(lane_mean(centered * centered) + LN_EPS)
    return centered * rate, rate


def norm_back(values, grad, gain):
    unit, rate = norm_parts(values)
    scaled = grad * gain
    d_values = rate * (scaled - lane_mean(scaled) - unit * lane_mean(scaled * unit))
    return (
        d_values,
        jnp.sum(grad * unit, axis=0, keepdims=True),
        jnp.sum(grad, axis=0, keepdims=True),
    )


def dot(left, right, dims=((1,), (0,))):
    return lax.dot_general(left, right, (dims, ((), ())), preferred_element_type=jnp.float32)


NT = ((1,), (1,))
TN = ((0,), (0,))


def allowed_mask(row_ref, col_ref, seg):
    row, col = row_ref[seg], col_ref[seg]
    return (row == col) | (row < 0) | (col < 0)


def forward_kernel(
    w_hbm, tok_ref, row_ref, col_ref, reset_ref, vec_ref, ext_ref, pos_ref,
    x_o, hc_o, proj_o, p_o, one_o, mid_o, gp_o, act_o, two_o, chosen_o,
    w, x, hc, proj, probs, one, mid, gp, act, two, mask, hid, final, sem_w, sem_o,
):
    bf, f32 = jnp.bfloat16, jnp.float32
    loads = [pltpu.make_async_copy(w_hbm.at[:, b], w.at[b], sem_w.at[b]) for b in range(12)]
    for load in loads:
        load.start()
    waited = set()

    def weight(b):
        if b not in waited:
            loads[b].wait()
            waited.add(b)
        return w[b].reshape(D, D)

    stores = []

    def store(src, dst):
        copy = pltpu.make_async_copy(src, dst, sem_o.at[len(stores)])
        copy.start()
        stores.append(copy)

    vec = [vec_ref[k : k + 1, :] for k in range(12)]
    b_q, b_v, b_o, g_one, b_one = vec[:5]
    b_up, b_down, g_two, b_two = vec[5:9], vec[9], vec[10], vec[11]
    gain_e, bias_e = ext_ref[404:405, :], ext_ref[405:406, :]
    lane = lax.broadcasted_iota(jnp.int32, (1, 2 * HD), 1)
    low_half = lane < HD
    for seg in range(SEGS):
        rows = pl.ds(seg * ROWS, ROWS)
        x[seg] = tok_ref[rows, :].astype(f32) + ext_ref[:ROWS, :]
        x[seg, ROWS - MEM :, :] += ext_ref[ROWS + MEM : ROWS + 2 * MEM, :]
        first = ext_ref[ROWS : ROWS + MEM, :]
        if seg == 0:
            x[seg, :MEM, :] += first
        else:
            x[seg, :MEM, :] += jnp.where(reset_ref[seg - 1] > 0, first, hid[ROWS - MEM :, :])
        store(x.at[seg], x_o.at[seg])
        mask[...] = allowed_mask(row_ref, col_ref, seg).astype(f32)
        unit, _ = norm_parts(x[seg])
        h = unit * gain_e + bias_e
        hid[...] = h
        h_low = h.astype(bf)
        hc[0, rows, :] = h_low
        for k, bias in ((0, b_q), (1, None), (2, b_v)):
            made = dot(h_low, weight(k))
            proj[k, rows, :] = (made if bias is None else made + bias).astype(bf)
        store(hc.at[0, rows], hc_o.at[0, rows])
        store(proj.at[:, rows], proj_o.at[:, rows])
        for pair in range(HEADS // 2):
            cols = pl.ds(pair * 2 * HD, 2 * HD)
            query, keyed, value = (proj[k, rows, cols] for k in range(3))
            query = query * jnp.asarray(HD ** (-0.5), bf)
            parts = []
            for side in range(2):
                keep = low_half if side == 0 else ~low_half
                scores = dot(jnp.where(keep, query, jnp.zeros_like(query)), keyed, NT)
                scores = jnp.where(mask[...] > 0, scores, MASKED)
                expd = jnp.exp(scores - jnp.max(scores, axis=-1, keepdims=True))
                p_low = (expd * (1.0 / jnp.sum(expd, axis=-1, keepdims=True))).astype(bf)
                probs[seg, pair * 2 + side] = p_low
                parts.append(dot(p_low, value))
            hc[1, rows, cols] = jnp.where(low_half, parts[0], parts[1]).astype(bf)
        store(probs.at[seg], p_o.at[seg])
        store(hc.at[1, rows], hc_o.at[1, rows])
        sum_one = hid[...] + (dot(hc[1, rows, :], weight(3)) + b_o)
        one[seg] = sum_one
        store(one.at[seg], one_o.at[seg])
        unit, _ = norm_parts(sum_one)
        mid_now = unit * g_one + b_one
        mid_low = mid_now.astype(bf)
        mid[rows, :] = mid_low
        store(mid.at[rows], mid_o.at[rows])
        for j in range(4):
            up = dot(mid_low, weight(4 + j)) + b_up[j]
            half = 0.5 * (1.0 + lax.erf(up * 0.7071067811865476))
            gp[j, rows, :] = (half + up * jnp.exp(-0.5 * up * up) * 0.3989422804014327).astype(bf)
            act[j, rows, :] = (up * half).astype(bf)
        store(gp.at[:, rows], gp_o.at[:, rows])
        store(act.at[:, rows], act_o.at[:, rows])
        total = mid_now + b_down
        for j in range(4):
            total = total + dot(act[j, rows, :], weight(8 + j))
        two[seg] = total
        store(two.at[seg], two_o.at[seg])
        unit, _ = norm_parts(total)
        h = unit * g_two + b_two
        hid[...] = h
        final[rows, :] = h.astype(bf)
    at = lax.broadcasted_iota(jnp.int32, (MLM_PAD, SEGS * ROWS), 1)
    chosen_o[...] = dot((at == pos_ref[...]).astype(bf), final[...]).astype(bf)
    for copy in stores:
        copy.wait()


def run_forward(w_all, tok, marks, reset, vec, ext, pos):
    f32, bf = jnp.float32, jnp.bfloat16
    n = SEGS * ROWS
    saved = [
        ((SEGS, ROWS, D), f32),
        ((2, n, D), bf),
        ((3, n, D), bf),
        ((SEGS, HEADS, ROWS, ROWS), bf),
        ((SEGS, ROWS, D), f32),
        ((n, D), bf),
        ((4, n, D), bf),
        ((4, n, D), bf),
        ((SEGS, ROWS, D), f32),
    ]
    hbm = pl.BlockSpec(memory_space=pl.ANY)
    vmem = pl.BlockSpec(memory_space=pltpu.VMEM)
    return pl.pallas_call(
        forward_kernel,
        out_shape=[jax.ShapeDtypeStruct(s, k) for s, k in saved]
        + [jax.ShapeDtypeStruct((MLM_PAD, D), bf)],
        in_specs=[hbm, vmem, vmem, vmem, pl.BlockSpec(memory_space=pltpu.SMEM), vmem, vmem, vmem],
        out_specs=[hbm] * len(saved) + [vmem],
        scratch_shapes=[pltpu.VMEM((12, w_all.shape[0]) + w_all.shape[2:], bf)]
        + [pltpu.VMEM(s, k) for s, k in saved]
        + [
            pltpu.VMEM((ROWS, ROWS), f32),
            pltpu.VMEM((ROWS, D), f32),
            pltpu.VMEM((n, D), bf),
            pltpu.SemaphoreType.DMA((12,)),
            pltpu.SemaphoreType.DMA((SEGS * 10,)),
        ],
        compiler_params=pltpu.CompilerParams(vmem_limit_bytes=60 << 20),
    )(w_all, tok, marks[:, None, :], marks[:, :, None], reset, vec, ext, pos[:, None])


def backward_kernel(
    cuts,
    w_hbm, x_i, hc_i, proj_i, p_i, one_i, mid_i, gp_i, act_i, two_i,
    dch_ref, reset_ref, vec_ref, ext_ref, pos_ref, give_ref, slot_ref, v_ref,
    share_o, small_o, dpack_o, dtok,
    w, x, hc, right, probs, one, mid, rup, act, two, rdown, grad, dmem, sem_w, sem_i,
):
    bf, f32 = jnp.bfloat16, jnp.float32
    small_o[...] = jnp.zeros_like(small_o)
    loads = {}
    state = {"n": 0}

    def load(name, src, dst):
        copy = pltpu.make_async_copy(src, dst, sem_i.at[state["n"]])
        state["n"] += 1
        copy.start()
        loads[name] = copy

    def need(name):
        if name in loads:
            loads.pop(name).wait()

    wl = [pltpu.make_async_copy(w_hbm.at[:, b], w.at[b], sem_w.at[b]) for b in range(12)]
    waited = set()

    def weight(b):
        if b not in waited:
            wl[b].wait()
            waited.add(b)
        return w[b].reshape(D, D)

    order = list(reversed(range(SEGS)))
    for i, seg in enumerate(order):
        rows = pl.ds(seg * ROWS, ROWS)
        load(("two", seg), two_i.at[seg], two.at[seg])
        if i == 0:
            for b in range(8, 12):
                wl[b].start()
        load(("gp", seg), gp_i.at[:, rows], rup.at[:, rows])
        if i == 0:
            for b in range(4, 8):
                wl[b].start()
        load(("one", seg), one_i.at[seg], one.at[seg])
        if i == 0:
            wl[3].start()
            load(("p", seg), p_i.at[seg], probs)
        load(("proj", seg), proj_i.at[:, rows], right.at[pl.ds(0, 3), rows])
        if i == 0:
            for b in range(3):
                wl[b].start()
        load(("x", seg), x_i.at[seg], x.at[seg])
    load("hc", hc_i, hc)
    load("mid", mid_i, mid)
    load("act", act_i, act)

    vec = [vec_ref[k : k + 1, :] for k in range(12)]
    g_one, g_two, gain_e = vec[3], vec[10], ext_ref[404:405, :]
    lane = lax.broadcasted_iota(jnp.int32, (1, 2 * HD), 1)
    low_half = lane < HD
    at = lax.broadcasted_iota(jnp.int32, (MLM_PAD, SEGS * ROWS), 1)
    at_pos = (at == pos_ref[...]).astype(bf)
    v0 = EXT

    def add_row(k, value):
        small_o[v0 + k : v0 + k + 1, :] += value

    def sums(values):
        return jnp.sum(values.astype(f32), axis=0, keepdims=True)

    for i, seg in enumerate(order):
        rows = pl.ds(seg * ROWS, ROWS)
        grad[...] = dot(at_pos[:, seg * ROWS : (seg + 1) * ROWS], dch_ref[...], TN)
        if i > 0:
            grad[ROWS - MEM :, :] += dmem[...]
        need(("two", seg))
        d_two, d_gain, d_shift = norm_back(two[seg], grad[...], g_two)
        add_row(10, d_gain)
        add_row(11, d_shift)
        r_down = d_two.astype(bf)
        rdown[rows, :] = r_down
        add_row(9, sums(r_down))
        need(("gp", seg))
        for j in range(4):
            r_up = (rup[j, rows, :].astype(f32) * dot(r_down, weight(8 + j), NT)).astype(bf)
            rup[j, rows, :] = r_up
            add_row(5 + j, sums(r_up))
        for j in range(4):
            d_two = d_two + dot(rup[j, rows, :], weight(4 + j), NT)
        need(("one", seg))
        d_one, d_gain, d_shift = norm_back(one[seg], d_two, g_one)
        add_row(3, d_gain)
        add_row(4, d_shift)
        grad[...] = d_one
        r_att = d_one.astype(bf)
        right[3, rows, :] = r_att
        add_row(2, sums(r_att))
        d_ctx = dot(r_att, weight(3), NT).astype(bf)
        need(("p", seg))
        need(("proj", seg))
        for pair in range(HEADS // 2):
            cols = pl.ds(pair * 2 * HD, 2 * HD)
            query, keyed, value = (right[k, rows, cols] for k in range(3))
            d_out = d_ctx[:, pair * 2 * HD : (pair + 1) * 2 * HD]
            made = []
            for side in range(2):
                keep = low_half if side == 0 else ~low_half
                p_low = probs[pair * 2 + side]
                p_now = p_low.astype(f32)
                d_p = dot(jnp.where(keep, d_out, jnp.zeros_like(d_out)), value, NT)
                weighted = p_now * d_p
                d_s = weighted - p_now * jnp.sum(weighted, axis=-1, keepdims=True)
                d_s = d_s.astype(bf)
                made.append((dot(d_s, keyed), dot(d_s, query, TN), dot(p_low, d_out, TN)))
            for k, scale in ((0, HD ** (-0.5)), (1, HD ** (-0.5)), (2, 1.0)):
                both = jnp.where(low_half, made[0][k], made[1][k]) * scale
                right[k, rows, cols] = both.astype(bf)
        if i + 1 < SEGS:
            load(("p", order[i + 1]), p_i.at[order[i + 1]], probs)
        d_h = grad[...]
        for k in range(3):
            d_h = d_h + dot(right[k, rows, :], weight(k), NT)
        add_row(0, sums(right[0, rows, :]))
        add_row(1, sums(right[2, rows, :]))
        need(("x", seg))
        d_x, d_gain, d_shift = norm_back(x[seg], d_h, gain_e)
        grad[...] = d_x
        dtok[rows, :] = d_x.astype(bf)
        small_o[:ROWS, :] += d_x
        small_o[ROWS + MEM : ROWS + 2 * MEM, :] += grad[ROWS - MEM :, :]
        small_o[404:405, :] += d_gain
        small_o[405:406, :] += d_shift
        d_read = grad[:MEM, :]
        if seg > 0:
            back = reset_ref[seg - 1] > 0
            small_o[ROWS : ROWS + MEM, :] += jnp.where(back, d_read, 0.0)
            dmem[...] = jnp.where(back, 0.0, d_read)
        else:
            small_o[ROWS : ROWS + MEM, :] += d_read
    dpack_o[...] = dot((give_ref[...] == slot_ref[...]).astype(bf), dtok[...]).astype(bf)
    need("hc")
    need("mid")
    need("act")
    v = v_ref[0]
    width = D // cuts
    block, cut = v // cuts, v % cuts
    cols = pl.ds(pl.multiple_of(cut * width, 128), width)
    share_o[0] = dot(hc[block // 3], right[block, :, cols], TN).astype(bf)
    share_o[1] = dot(mid[...], rup[block, :, cols], TN).astype(bf)
    share_o[2] = dot(act[block], rdown[:, cols], TN).astype(bf)


def run_backward(
    w_all, saved, d_chosen, reset, vec, ext, pos, give, slot, v_idx, cuts, small_rows
):
    f32, bf = jnp.float32, jnp.bfloat16
    n = SEGS * ROWS
    hbm = pl.BlockSpec(memory_space=pl.ANY)
    vmem = pl.BlockSpec(memory_space=pltpu.VMEM)
    smem = pl.BlockSpec(memory_space=pltpu.SMEM)
    return pl.pallas_call(
        functools.partial(backward_kernel, cuts),
        out_shape=[
            jax.ShapeDtypeStruct((3, D, D // cuts), bf),
            jax.ShapeDtypeStruct((small_rows, D), f32),
            jax.ShapeDtypeStruct((give.shape[0], D), bf),
            jax.ShapeDtypeStruct((n, D), bf),
        ],
        in_specs=[hbm] * 10 + [vmem, smem, vmem, vmem, vmem, vmem, vmem, smem],
        out_specs=[vmem] * 4,
        scratch_shapes=[
            pltpu.VMEM((12, w_all.shape[0]) + w_all.shape[2:], bf),
            pltpu.VMEM((SEGS, ROWS, D), f32),
            pltpu.VMEM((2, n, D), bf),
            pltpu.VMEM((4, n, D), bf),
            pltpu.VMEM((HEADS, ROWS, ROWS), bf),
            pltpu.VMEM((SEGS, ROWS, D), f32),
            pltpu.VMEM((n, D), bf),
            pltpu.VMEM((4, n, D), bf),
            pltpu.VMEM((4, n, D), bf),
            pltpu.VMEM((SEGS, ROWS, D), f32),
            pltpu.VMEM((n, D), bf),
            pltpu.VMEM((ROWS, D), f32),
            pltpu.VMEM((MEM, D), f32),
            pltpu.SemaphoreType.DMA((12,)),
            pltpu.SemaphoreType.DMA((SEGS * 6 + 4,)),
        ],
        compiler_params=pltpu.CompilerParams(vmem_limit_bytes=61 << 20),
    )(
        w_all, *saved, d_chosen, reset, vec, ext, pos[:, None],
        give[:, None], slot[None, :], v_idx,
    )


def ceil_to(value, unit):
    return -(-value // unit) * unit


def per_device(
    ids,
    docs,
    resets,
    mlm_pos,
    mlm_label,
    step,
    qkv_master,
    qkv_first,
    qkv_second,
    out_master,
    out_first,
    out_second,
    up_master,
    up_first,
    up_second,
    down_master,
    down_first,
    down_second,
    embed_master,
    embed_first,
    embed_second,
    vectors_master,
    vectors_first,
    vectors_second,
    extras_master,
    extras_first,
    extras_second,
):
    f32, bf = jnp.float32, jnp.bfloat16
    n_dp = lax.axis_size("dp")
    n_v = lax.axis_size("vocab")
    d_idx = lax.axis_index("dp")
    v_idx = lax.axis_index("vocab")
    count = n_dp * MLM
    own_rows = embed_master.shape[0]
    tokens_n = SEGS * SEG
    rb = qkv_master.shape[1]
    cuts = max(1, n_v // 4)
    width = D // cuts
    groups = 12 * cuts // n_v

    def to_blocks(qkv, out, up, down):
        full = jnp.concatenate(
            [
                qkv[0].reshape(rb, 3, D).transpose(1, 0, 2),
                out,
                up[0].reshape(rb, n_dp, 4, rb).transpose(2, 0, 1, 3).reshape(4, rb, D),
                down[0].reshape(4, rb, D),
            ]
        )
        return full.reshape(12, rb, cuts, width).transpose(0, 2, 1, 3).reshape(12 * cuts, rb, width)

    def from_blocks(blocks):
        full = blocks.reshape(12, cuts, rb, width).transpose(0, 2, 1, 3).reshape(12, rb, D)
        return (
            full[:3].transpose(1, 0, 2).reshape(1, rb, 3 * D),
            full[3:4],
            full[4:8].reshape(4, rb, n_dp, rb).transpose(1, 2, 0, 3).reshape(1, rb, FF),
            full[8:].reshape(1, 4 * rb, D),
        )

    ids_all = lax.all_gather(ids, "dp", axis=0, tiled=True)
    labels = jnp.full((n_dp, MLM_PAD - MLM), -1, jnp.int32)
    labels_all = jnp.concatenate([lax.all_gather(mlm_label, "dp", axis=0, tiled=True), labels], axis=1)
    holder = ids_all // own_rows
    local_row = ids_all % own_rows
    order = jnp.arange(tokens_n, dtype=jnp.int32)
    same = (holder[:, :, None] == holder[:, None, :]) & (order[None, :, None] > order[None, None, :])
    rank = jnp.sum(same.astype(jnp.int32), axis=-1)
    cap = ceil_to(2 * tokens_n // (n_dp * n_v) + 2, 16)
    overflow = jnp.max(rank) >= cap
    mine = holder == d_idx * n_v + v_idx
    places = jnp.arange(cap, dtype=jnp.int32)
    hit = mine[:, None, :] & (rank[:, None, :] == places[None, :, None])
    packed_row = jnp.sum(jnp.where(hit, local_row[:, None, :] + 1, 0), axis=-1) - 1
    own_slots = jnp.arange(own_rows, dtype=jnp.int32)
    pick = (packed_row.reshape(n_dp * cap)[:, None] == own_slots[None, :]).astype(bf)
    table = embed_master.astype(bf)
    packed = jnp.dot(pick, table, preferred_element_type=f32).astype(bf).reshape(n_dp, cap, D)

    blocks = to_blocks(
        qkv_master.astype(bf), out_master.astype(bf), up_master.astype(bf), down_master.astype(bf)
    )
    w_all, tok_all = gather_weights(blocks, packed, n_dp, n_v)
    if cuts > 1 or rb % 16:
        w_all = w_all.reshape(n_dp, 12, cuts, rb, width).transpose(1, 0, 3, 2, 4).reshape(1, 12, D, D)

    my_holder = holder[d_idx]
    my_rank = rank[d_idx]
    slot = (my_holder * cap + my_rank).reshape(SEGS, SEG)
    slot = jnp.pad(slot, ((0, 0), (MEM, MEM)), constant_values=-1).reshape(SEGS * ROWS)

    def packed_tokens(_):
        slots = jnp.arange(n_dp * n_v * cap, dtype=jnp.int32)
        onehot = (slot[:, None] == slots[None, :]).astype(bf)
        rows = tok_all.reshape(n_dp * n_v * cap, D)
        return jnp.dot(onehot, rows, preferred_element_type=f32).astype(bf)

    def whole_tokens(_):
        whole = lax.all_gather(table, "dp", axis=0, tiled=True)
        at = jnp.arange(n_dp * own_rows, dtype=jnp.int32)
        row_ids = (at // own_rows * n_v + v_idx) * own_rows + at % own_rows
        onehot = (ids[0][:, None] == row_ids[None, :]).astype(bf)
        rows = lax.psum(jnp.dot(onehot, whole, preferred_element_type=f32).astype(bf), "vocab")
        return jnp.pad(rows.reshape(SEGS, SEG, D), ((0, 0), (MEM, MEM), (0, 0))).reshape(-1, D)

    tokens = lax.cond(overflow, whole_tokens, packed_tokens, 0)
    marks = jnp.pad(docs.reshape(SEGS, SEG), ((0, 0), (MEM, MEM)), constant_values=-1)
    vec = vectors_master[0].reshape(12, D)
    b_up = vec[5:9].reshape(n_dp, 4, rb).transpose(1, 0, 2).reshape(4, D)
    vec = jnp.concatenate([vec[:5], b_up, vec[9:]])
    positions = mlm_pos[0]
    at_rows = positions // SEG * ROWS + MEM + positions % SEG
    at_rows = jnp.concatenate([at_rows, jnp.full((MLM_PAD - MLM,), -1, jnp.int32)])
    *saved, chosen = run_forward(w_all, tokens, marks, resets[0], vec, extras_master, at_rows)
    rows_v = MLM_PAD // n_v
    chosen_all = gather_chosen(chosen.reshape(n_v, rows_v, D), n_dp, n_v).reshape(n_dp * MLM_PAD, D)

    logits = jnp.einsum("md,vd->mv", chosen_all, table, preferred_element_type=f32)
    row_ids = (d_idx * n_v + v_idx) * own_rows + own_slots
    label_flat = labels_all.reshape(n_dp * MLM_PAD)
    hits = label_flat[:, None] == row_ids[None, :]
    top = lax.pmax(jnp.max(logits, axis=-1), ("dp", "vocab"))
    sums, target = lax.psum(
        (
            jnp.sum(jnp.exp(logits - top[:, None]), axis=-1),
            jnp.sum(jnp.where(hits, logits, 0.0), axis=-1),
        ),
        ("dp", "vocab"),
    )
    lse = top + jnp.log(sums)
    real = label_flat >= 0
    loss = jnp.sum(jnp.where(real, lse - target, 0.0)) / count
    d_logits = ((jnp.exp(logits - lse[:, None]) - hits.astype(f32)) / count).astype(bf)
    d_table = jnp.einsum("mv,md->vd", d_logits, chosen_all, preferred_element_type=f32)
    d_part = jnp.dot(d_logits, table, preferred_element_type=f32).astype(bf)
    d_chosen = reduce_d_chosen(
        d_part.reshape(n_dp // 2, 2, n_v // 2, 2, rows_v, D), n_dp, n_v
    ).reshape(MLM_PAD, D)
    small_rows = EXT + 12
    e_rows = ceil_to(-(-small_rows // (n_dp * n_v)), 16)
    at = jnp.arange(n_dp * cap, dtype=jnp.int32)
    give = (at // cap * n_v + v_idx) * cap + at % cap
    shares, small, d_packed, d_tok = run_backward(
        w_all,
        saved,
        d_chosen,
        resets[0],
        vec,
        extras_master,
        at_rows,
        give,
        slot,
        v_idx[None],
        cuts,
        ceil_to(small_rows, 8),
    )
    shares = shares.reshape(groups, n_dp // 2, 2, rb, width)
    small = jnp.pad(small.astype(bf), ((0, e_rows * n_dp * n_v - small.shape[0]), (0, 0)))
    small = small.reshape(n_dp // 2, 2, n_v, e_rows, D)
    small = lax.dynamic_index_in_dim(small, v_idx, axis=2, keepdims=False)
    d_packed = d_packed.reshape(n_dp, cap, D)
    g_blocks, small_all, d_packed_all = reduce_grads(shares, small, d_packed, n_dp, n_v)

    def packed_d_table(_):
        return jnp.einsum(
            "tv,td->vd", pick, d_packed_all.reshape(n_dp * cap, D), preferred_element_type=f32
        )

    def whole_d_table(_):
        d_all = d_tok.reshape(SEGS, ROWS, D)[:, MEM : MEM + SEG].reshape(tokens_n, D)
        d_all = lax.all_gather(d_all, "dp", axis=0, tiled=True)
        onehot = (ids_all.reshape(-1)[:, None] == row_ids[None, :]).astype(bf)
        return jnp.einsum("tv,td->vd", onehot, d_all, preferred_element_type=f32)

    s_table = d_table + lax.cond(overflow, whole_d_table, packed_d_table, 0)
    s_qkv, s_out, s_up, s_down = from_blocks(g_blocks.astype(f32))
    small_all = small_all.astype(f32).reshape(n_dp * n_v * e_rows, D)
    g_ext = small_all[: extras_master.shape[0]]
    g_vec = small_all[EXT:small_rows]
    g_up_bias = g_vec[5:9].reshape(4, n_dp, rb).transpose(1, 0, 2).reshape(4, D)
    g_vec = jnp.concatenate([g_vec[:5], g_up_bias, g_vec[9:]]).reshape(vectors_master.shape)

    layer_sq = jnp.where(v_idx == 0, squares((s_qkv, s_out, s_up, s_down)), 0.0)
    small_sq = jnp.where((v_idx == 0) & (d_idx == 0), squares((g_vec, g_ext)), 0.0)
    norm = jnp.sqrt(lax.psum(layer_sq + squares((s_table,)) + small_sq, ("dp", "vocab")))
    coef = jnp.minimum(1.0, CLIP / (norm + 1e-06))
    step_count = step[0].astype(f32)
    results = [loss, norm]
    for master, first, second, grad, rate in (
        (qkv_master, qkv_first, qkv_second, s_qkv, LR_BIG),
        (out_master, out_first, out_second, s_out, LR_BIG),
        (up_master, up_first, up_second, s_up, LR_BIG),
        (down_master, down_first, down_second, s_down, LR_BIG),
        (embed_master, embed_first, embed_second, s_table, LR_BIG),
        (vectors_master, vectors_first, vectors_second, g_vec, LR_SMALL),
        (extras_master, extras_first, extras_second, g_ext, LR_SMALL),
    ):
        results.extend(adam(master, first, second, grad, coef, step_count, rate))
    return tuple(results)


def solution(mesh):
    in_specs = (
        P("dp", None),
        P("dp", None),
        P("dp", None),
        P("dp", None),
        P("dp", None),
        P(),
        P(None, "dp", None),
        P(None, "dp", None),
        P(None, "dp", None),
        P(None, "dp", None),
        P(None, "dp", None),
        P(None, "dp", None),
        P(None, "dp", None),
        P(None, "dp", None),
        P(None, "dp", None),
        P(None, "dp", None),
        P(None, "dp", None),
        P(None, "dp", None),
        P(("dp", "vocab"), None),
        P(("dp", "vocab"), None),
        P(("dp", "vocab"), None),
        P(),
        P(),
        P(),
        P(),
        P(),
        P(),
    )
    out_specs = (
        P(),
        P(),
        P(None, "dp", None),
        P(None, "dp", None),
        P(None, "dp", None),
        P(None, "dp", None),
        P(None, "dp", None),
        P(None, "dp", None),
        P(None, "dp", None),
        P(None, "dp", None),
        P(None, "dp", None),
        P(None, "dp", None),
        P(None, "dp", None),
        P(None, "dp", None),
        P(("dp", "vocab"), None),
        P(("dp", "vocab"), None),
        P(("dp", "vocab"), None),
        P(),
        P(),
        P(),
        P(),
        P(),
        P(),
    )
    return jax.shard_map(
        per_device, mesh=mesh, in_specs=in_specs, out_specs=out_specs, check_vma=False
    )
```

time: 1520 us -> 614 us (0.40)
  waiting for transfers between devices: 1100 us -> 0 us
  Pallas kernels: 0 us -> 320 us
  matrix products: 177 us -> 17.6 us
  blocking collectives: 90.4 us -> 168 us
  other arithmetic: 71.4 us -> 40.8 us
  local copies, waits for them, and re-layouts: 46.1 us -> 25.5 us
    reduce_scatter x5 -> x0, waiting for transfers between devices: 709 us -> none  [the longest x1 196 us: per_device(): lax.psum_scatter(g_table, 'dp', scatter_dimension=0, tiled=True)]
    all_gather x5 -> x0, waiting for transfers between devices: 338 us -> none  [the longest x1 98 us: per_device(): lax.all_gather(embed_master.astype(jnp.bfloat16), 'dp', axis=0, tiled=True)]
    pallas_call x0 -> x6, Pallas kernels: none -> 320 us  [the longest x1 98.7 us: gather_weights(): pl.pallas_call(functools.partial(weights_kernel, n_dp, n_v), out_shape=(j...]
    dot_general x41 -> x6, matrix products: 177 us -> 17.6 us  [the longest x1 4.94 us: per_device(): jnp.einsum('mv,md->vd', d_logits, chosen_all, preferred_element_type=f32)]
    psum x3 -> x0, waiting for transfers between devices: 56 us -> none  [the longest x1 30 us: run_item(): lax.psum(jnp.einsum('mv,vd->md', d_logits, table, preferred_element_type=...]
    all_gather x0 -> x2, blocking collectives: none -> 51.8 us  [the longest x1 32.4 us: per_device(): ids_all = lax.all_gather(ids, 'dp', axis=0, tiled=True)]
    pmax x1, blocking collectives: 5.67 us -> 40.4 us  [per_device(): top = lax.pmax(jnp.max(logits, axis=-1), ('dp', 'vocab'))]
    unnamed x404 -> x89, local copies, waits for them, and re-layouts: 21.9 us -> 5.37 us
  transfers between devices with their start and end apart: 13 -> 0, of which waited for: 12 -> 0; matrix products, arithmetic and copies ran while one was open for 7% -> 0% of each run, Pallas kernels for 0% -> 0%
where the time goes in v1:
time: 614 us; the launch traced here: 606 us
  Pallas kernels  320 us (52%)
  blocking collectives  168 us (27%)
  other arithmetic  40.8 us (7%)
  local copies, waits for them, and re-layouts  25.5 us (4%)
  between operations  25.1 us (4%)
  matrix products  17.6 us (3%)
  loops' own time  9.22 us (2%)
    pallas_call x1, Pallas kernels, gather_weights(): pl.pallas_call(functools.partial(weights_kernel, n_dp, n_v), out_shape=(j...  98.7 us
    pallas_call x1, Pallas kernels, reduce_grads(): pl.pallas_call(functools.partial(grads_kernel, n_dp, n_v), out_shape=(jax...  85.5 us
    psum x2, blocking collectives, per_device(): lax.psum((jnp.sum(jnp.exp(logits - top[:, None]), axis=-1), jnp.sum(jnp.w...  75.9 us
    pallas_call x1, Pallas kernels, run_backward(): pl.pallas_call(functools.partial(backward_kernel, cuts), out_shape=[jax.S...  44.7 us
    pmax x1, blocking collectives, per_device(): top = lax.pmax(jnp.max(logits, axis=-1), ('dp', 'vocab'))  40.4 us
    pallas_call x1, Pallas kernels, run_forward(): pl.pallas_call(forward_kernel, out_shape=[jax.ShapeDtypeStruct(s, k) for...  34.7 us
    pallas_call x1, Pallas kernels, reduce_d_chosen(): pl.pallas_call(functools.partial(d_chosen_kernel, n_dp, n_v), out_shape=j...  33.1 us
    all_gather x1, blocking collectives, per_device(): ids_all = lax.all_gather(ids, 'dp', axis=0, tiled=True)  32.4 us

profile of v1, /device:TPU:0, one launch (start us, length us, event | category | flops | bytes accessed | tf_op | source)
XLA Modules:
  0.0 606.1 jit_solution(11457209214126982645)
XLA Ops:
  7.2 32.4 %all-gather.1 = s32[8,1,728]{2,1,0:T(1,128)S(1)} all-gather(s32[1,1,728]{2,1,0:T(1,128)} %bitcast.124), channel_id=1, replica_groups=mesh['dp'=8,'vocab'=4] {'dp'}, dimensions={0}, use_global_device_ids=true | all-gather | bytes 26208 | tf_op jit(solution)/shard_map/all_gather | solution.py:895
  39.8 4.4 convert_reduce_fusion
  52.0 98.7 %shard_map.434 = (bf16[8,12,96,768]{3,2,1,0:T(8,128)(2,1)}, bf16[8,4,48,768]{3,2,1,0:T(8,128)(2,1)}) custom-call(bf16[12,96,768]{2,1,0:T(8,128)(2,1)} %pad_maximum_fusion.w_ref, bf16[8,48,768]{2,1,0:T(8,128)(2,1)} %bitcast.115), custom_call_target="tpu_custom_call" | custom-call | tf_op jit(solution)/shard_map/pallas_call | solution.py:249
  152.1 12.7 %conditional.2 = (bf16[768,768]{1,0:T(8,128)(2,1)S(1)}) conditional(s32[]{:T(128)} %convert_element_type.68, (s32[2,384]{1,0:T(2,128)S(1)}, bf16[8,4,48,768]{3,2,1,0:T(8,128)(2,1)}) %tuple.20, (s32[1,728]{1,0:T(1,128)S(1)}, s32[]{:T(128)}, bf16[480,768]{1,0:T(8,128)(2,1)}) %tuple.61), branch_computations={%region_3.4_spmd, %region_4.6_spmd} | conditional | flops 4297893888 | bytes 38230656 | solution.py:940
  152.1 3.8 fusion.2
  168.6 34.7 %shard_map.435 = (f32[2,384,768]{2,1,0:T(8,128)}, bf16[2,768,768]{2,1,0:T(8,128)(2,1)}, bf16[3,768,768]{2,1,0:T(8,128)(2,1)}, bf16[2,12,384,384]{3,2,1,0:T(8,128...) custom-call(bf16[8,12,96,768]{3,2,1,0:T(8,128)(2,1)} %get-tuple-elem, ...), custom_call_target="tpu_custom_call" | custom-call | tf_op jit(solution)/shard_map/pallas_call | solution.py:617
  203.3 23.3 %shard_map.436 = bf16[8,4,32,768]{3,2,1,0:T(8,128)(2,1)} custom-call(bf16[4,32,768]{2,1,0:T(8,128)(2,1)} %bitcast.116), custom_call_target="tpu_custom_call" | custom-call | tf_op jit(solution)/shard_map/pallas_call | solution.py:282
  229.0 40.4 %pmax.7 = f32[1024]{0:T(1024)S(1)} all-reduce(f32[1024]{0:T(1024)S(1)} %get-tuple-element.137), channel_id=1, replica_groups=mesh['dp'=8,'vocab'=4] {'dp','vocab'}, use_global_device_ids=true, to_apply=%region_7.8 | all-reduce | flops 1024 | bytes 8192 | tf_op jit(solution)/shard_map/pmax | solution.py:956
  269.4 19.4 %all-gather = s32[8,1,112]{2,1,0:T(1,128)S(1)} all-gather(s32[1,1,112]{2,1,0:T(1,128)S(1)} %bitcast.125), channel_id=1, replica_groups=mesh['dp'=8,'vocab'=4] {'dp'}, dimensions={0}, use_global_device_ids=true | all-gather | bytes 4032 | tf_op jit(solution)/shard_map/all_gather | solution.py:897
  289.9 36.9 %psum.28 = f32[1024]{0:T(1024)S(1)} all-reduce(f32[1024]{0:T(1024)S(1)} %get-tuple-element.105), channel_id=1, replica_groups=mesh['dp'=8,'vocab'=4] {'dp','vocab'}, use_global_device_ids=true, to_apply=%region_9.10 | all-reduce | flops 1024 | bytes 8192 | tf_op jit(solution)/shard_map/psum | solution.py:957
  329.1 33.1 %shard_map.437 = bf16[4,32,768]{2,1,0:T(8,128)(2,1)} custom-call(bf16[4,2,2,2,32,768]{5,4,3,2,1,0:T(8,128)(2,1)} %bitcast.108), custom_call_target="tpu_custom_call" | custom-call | tf_op jit(solution)/shard_map/pallas_call | solution.py:339
  363.5 44.7 %shard_map.438 = (bf16[3,768,768]{2,1,0:T(8,128)(2,1)}, f32[424,768]{1,0:T(8,128)}, bf16[384,768]{1,0:T(8,128)(2,1)}, bf16[768,768]{1,0:T(8,128)(2,1)}) custom-call(bf16[8,12,96,768]{3,2,1,0:T(8,128)(2,1)} %get-tuple-element.83.w_hbm, f32[2,384,768]{2,1,0:T(8,128)} %get-tuple-element.86.x_i, bf16[2,768,768]{2,1,0:T(8,128)(2,1)} %get-tuple-element.87.hc_i, ...), custom_call_target="tpu_custom_call" | custom-call | tf_op jit(solution)/shard_map/pallas_call | solution.py:795
  410.3 85.5 %shard_map.439 = (bf16[12,96,768]{2,1,0:T(8,128)(2,1)}, bf16[8,4,16,768]{3,2,1,0:T(8,128)(2,1)}, bf16[8,48,768]{2,1,0:T(8,128)(2,1)}) custom-call(bf16[3,4,2,96,768]{4,3,2,1,0:T(8,128)(2,1)} %bitcast.102, bf16[4,2,16,768]{3,2,1,0:T(8,128)(2,1)} %dynamic-slice_bitcast_fusion.e_ref, bf16[8,48,768]{2,1,0:T(8,128)(2,1)} %bitcast.114), custom_call_target="tpu_custom_call" | custom-call | tf_op jit(solution)/shard_map/pallas_call | solution.py:444
  506.8 3.1 conditional.3
  506.8 2.8 fusion.66
  509.9 4.9 multiply_reduce_fusion
  520.9 39.1 %all-reduce.6 = (f32[1024]{0:T(1024)}, f32[]{:T(128)}) all-reduce(f32[1024]{0:T(1024)S(1)} %copy-done.33, f32[]{:T(128)S(6)} %add.321), channel_id=1, replica_groups=mesh['dp'=8,'vocab'=4] {'dp','vocab'}, use_global_device_ids=true, to_apply=%region_11.12 | all-reduce | flops 1025 | bytes 8200 | tf_op jit(solution)/shard_map/psum | solution.py:957
  561.5 5.0 multiply_subtract_fusion.1
  567.6 2.8 multiply_subtract_fusion
  572.0 2.9 mul.625
  574.9 3.6 copy.98
  578.5 3.6 mul.627
  582.1 4.9 multiply_subtract_fusion.3
  592.2 3.3 multiply_subtract_fusion.4
  (162 shorter events, 41.8 us)
Async XLA Ops:
  7.2 38.5 %copy-start.1 = (f32[480,768]{1,0:T(8,128)S(1)}, f32[480,768]{1,0:T(8,128)}, u32[]{:S(2)}) copy-start(f32[480,768]{1,0:T(8,128)} %param.49) | copy-start | bytes 4423684
  39.6 6.2 %copy-start.19 = (s32[8,1,728]{2,1,0:T(1,128)}, s32[8,1,728]{2,1,0:T(1,128)S(1)}, u32[]{:S(2)}) copy-start(s32[8,1,728]{2,1,0:T(1,128)S(1)} %all-gather.1) | copy-start | bytes 69892
  52.0 100.0 %copy-start.38 = (s32[1,728]{1,0:T(1,128)S(1)}, s32[1,728]{1,0:T(1,128)}, u32[]{:S(2)}) copy-start(s32[1,728]{1,0:T(1,128)} %param.31) | copy-start | bytes 8740
  152.0 14.2 %copy-start.24 = (f32[1,9216]{1,0:T(1,128)S(1)}, f32[1,9216]{1,0:T(1,128)}, u32[]{:S(2)}) copy-start(f32[1,9216]{1,0:T(1,128)} %param.52) | copy-start | bytes 110596
  152.0 15.2 %copy-start.44 = (s32[1,112]{1,0:T(1,128)S(1)}, s32[1,112]{1,0:T(1,128)}, u32[]{:S(2)}) copy-start(s32[1,112]{1,0:T(1,128)} %param.34) | copy-start | bytes 1348
  203.3 23.3 %copy-start.10 = (bf16[480,768]{1,0:T(8,128)(2,1)S(1)}, bf16[480,768]{1,0:T(8,128)(2,1)}, u32[]{:S(2)}) copy-start(bf16[480,768]{1,0:T(8,128)(2,1)} %copy-done.9) | copy-start | bytes 2211844
  226.6 42.8 %copy-start.43 = (s32[1,112]{1,0:T(1,128)S(1)}, s32[1,112]{1,0:T(1,128)}, u32[]{:S(2)}) copy-start(s32[1,112]{1,0:T(1,128)} %param.35) | copy-start | bytes 1348
  269.4 59.7 %copy-start.40 = (s32[480]{0:T(512)}, s32[480]{0:T(512)S(1)}, u32[]{:S(2)}) copy-start(s32[480]{0:T(512)S(1)} %iota_add_fusion) | copy-start | bytes 5764
  288.8 40.3 %copy-start.29 = (s32[8,1,112]{2,1,0:T(1,128)}, s32[8,1,112]{2,1,0:T(1,128)S(1)}, u32[]{:S(2)}) copy-start(s32[8,1,112]{2,1,0:T(1,128)S(1)} %all-gather) | copy-start | bytes 10756
  288.8 40.3 %copy-start.34 = (s32[1024]{0:T(1024)}, s32[1024]{0:T(1024)S(1)}, u32[]{:S(2)}) copy-start(s32[1024]{0:T(1024)S(1)} %pad_bitcast_fusion) | copy-start | bytes 12292
  497.1 9.7 %copy-start = (f32[512,768]{1,0:T(8,128)}, f32[512,768]{1,0:T(8,128)S(1)}, u32[]{:S(2)}) copy-start(f32[512,768]{1,0:T(8,128)S(1)} %bitcast_convert_fusion) | copy-start | bytes 4718596
  509.9 5.0 copy-start.11
  561.4 5.1 copy-start.23
  561.4 5.1 copy-start.27
  561.4 5.2 copy-start.25
  561.5 5.2 copy-start.31
  561.5 5.2 copy-start.32
  561.5 6.1 %copy-start.2 = (f32[480,768]{1,0:T(8,128)S(1)}, f32[480,768]{1,0:T(8,128)}, u32[]{:S(2)}) copy-start(f32[480,768]{1,0:T(8,128)} %param.49) | copy-start | bytes 4423684
  561.5 6.1 copy-start.12
  561.5 6.0 copy-start.13
  561.5 6.0 copy-start.14
  582.1 4.9 copy-start.6
  582.1 4.9 copy-start.15
  582.1 4.9 copy-start.16
  (19 other events, 42.6 us)

commit v2 on v1

--- a/solution.py
+++ b/solution.py
@@ -30,23 +30,6 @@
 MASKED = -1000000000.0
 
 
-def squares(arrays):
-    total = jnp.zeros((), jnp.float32)
-    for values in arrays:
-        total = total + jnp.sum(values * values)
-    return total
-
-
-def adam(master, first, second, grad, coef, count, rate):
-    clipped = grad * coef
-    first_new = BETA_ONE * first + (1.0 - BETA_ONE) * clipped
-    second_new = BETA_TWO * second + (1.0 - BETA_TWO) * clipped * clipped
-    first_hat = first_new / (1.0 - BETA_ONE**count)
-    second_hat = second_new / (1.0 - BETA_TWO**count)
-    master_new = master - rate * (first_hat / (jnp.sqrt(second_hat) + ADAM_EPS) + DECAY * master)
-    return (master_new, first_new, second_new)
-
-
 MESH = pl.DeviceIdType.MESH
 MLM_PAD = 128
 EXT = ROWS + 2 * MEM + 2
@@ -108,8 +91,9 @@
 
 
 class Gather:
-    def __init__(self, place, copies, base, ref, own=None):
+    def __init__(self, place, copies, base, ref, own=None, shared=False):
         self.p, self.q, self.base, self.ref, self.own = place, copies, base, ref, own
+        self.least = 1 if shared else 0
         A, Y = place.A, place.Y
         self.x0 = base + A - 1
         self.y0 = self.x0 + A
@@ -133,6 +117,8 @@
         src = self.at(slot) if (slot or self.own is None) else self.own
         if slot < p.A:
             self.q.send(self.x0 + slot, src, self.at(slot), p.xp)
+        if slot < self.least:
+            return
         for k in range(1, p.Y):
             self.q.send(self.y0 + slot * (p.Y - 1) + k - 1, src, self.at(slot), p.yp(k))
         self.q.send(self.c0 + slot * p.Y, src, self.at(slot), p.cp)
@@ -157,14 +143,14 @@
 
     def step_y(self):
         p = self.p
-        for slot in range(2 * p.A):
+        for slot in range(self.least, 2 * p.A):
             for j in range(1, p.Y):
                 self.q.arrived(self.y0 + slot * (p.Y - 1) + j - 1, self.at(slot, j))
                 self.q.send(self.c0 + slot * p.Y + j, self.at(slot, j), self.at(slot, j), p.cp)
 
     def step_c(self):
         p = self.p
-        for slot in range(2 * p.A):
+        for slot in range(self.least, 2 * p.A):
             for j in range(p.Y):
                 self.q.arrived(self.c0 + slot * p.Y + j, self.at(slot, j, 1 - p.c))
 
@@ -182,18 +168,17 @@
     locals_ = [local]
     gathers = []
     base = 0
+    own = pltpu.make_async_copy(w_ref, out_ref.at[p.d], ls.at[1])
+    own.start()
+    locals_.append(own)
     for g in range(groups):
-        own = pltpu.make_async_copy(
-            w_ref.at[g * n_v + p.v], out_ref.at[p.d, g * n_v + p.v], ls.at[1 + g]
-        )
-        own.start()
-        locals_.append(own)
         gather = Gather(
             p,
             q,
             base,
             lambda d, v, g=g: out_ref.at[d, g * n_v + v],
             own=w_ref.at[g * n_v + p.v],
+            shared=True,
         )
         base = gather.end
         gathers.append(gather)
@@ -257,48 +242,115 @@
         scratch_shapes=[
             pltpu.SemaphoreType.DMA((count,)),
             pltpu.SemaphoreType.DMA((count,)),
-            pltpu.SemaphoreType.DMA((1 + groups,)),
+            pltpu.SemaphoreType.DMA((2,)),
         ],
         compiler_params=pltpu.CompilerParams(collective_id=0, has_side_effects=True),
     )(blocks, packed)
 
 
-def chosen_kernel(n_dp, n_v, in_ref, out_ref, ss, rs):
+def ints_kernel(n_dp, in_ref, out_ref, ss, rs):
+    d, v = lax.axis_index("dp"), lax.axis_index("vocab")
+    sem = pltpu.get_barrier_semaphore()
+    for k in range(1, n_dp):
+        partner = (lax.rem(d + k, n_dp), v)
+        pl.semaphore_signal(sem, 1, device_id=partner, device_id_type=MESH)
+    pl.semaphore_wait(sem, n_dp - 1)
+    q = Copies((d, v), ss, rs)
+    for k in range(1, n_dp):
+        q.send(k - 1, in_ref, out_ref.at[d], (lax.rem(d + k, n_dp), v))
+    out_ref[d] = in_ref[...]
+    for k in range(1, n_dp):
+        q.arrived(k - 1, out_ref.at[lax.rem(d + n_dp - k, n_dp)])
+    q.finish()
+
+
+def gather_ints(values, n_dp):
+    return pl.pallas_call(
+        functools.partial(ints_kernel, n_dp),
+        out_shape=jax.ShapeDtypeStruct((n_dp,) + values.shape, values.dtype),
+        in_specs=[pl.BlockSpec(memory_space=pltpu.VMEM)],
+        out_specs=pl.BlockSpec(memory_space=pltpu.VMEM),
+        scratch_shapes=[pltpu.SemaphoreType.DMA((n_dp - 1,)), pltpu.SemaphoreType.DMA((n_dp - 1,))],
+        compiler_params=pltpu.CompilerParams(collective_id=1, has_side_effects=True),
+    )(values)
+
+
+def head_kernel(
+    n_dp, n_v, ch_ref, table_ref, label_ref, tags_ref,
+    out_ref, dtab_ref, loss_ref,
+    al, logits, dlog, st, sd, sv, lse_s, part, bc, by, bx, bz, pc, py, px, ss, rs,
+):
+    f32, bf = jnp.float32, jnp.bfloat16
     p = Place(n_dp, n_v)
-    p.barrier()
+    A, Y = p.A, p.Y
+    count = n_dp * MLM
+    others = [(lax.rem(p.d + k, n_dp), p.v) for k in range(1, n_dp)]
+    partners = [(p.d, lax.rem(p.v + k, n_v)) for k in range(1, n_v)]
+    sem = pltpu.get_barrier_semaphore()
+    for partner in others + partners:
+        pl.semaphore_signal(sem, 1, device_id=partner, device_id_type=MESH)
+    pl.semaphore_wait(sem, n_dp - 1 + n_v - 1)
     q = Copies(p.me, ss, rs)
-    gather = Gather(p, q, 0, lambda d, v: out_ref.at[d, v])
-    out_ref[p.d, p.v] = in_ref[p.v]
+    gather = Gather(p, q, 0, lambda d, v: al.at[d, v], shared=True)
+    al[p.d] = ch_ref[...]
     gather.start()
     gather.step_a()
     gather.step_x()
     gather.step_y()
     gather.step_c()
-    q.finish()
-
-
-def gather_chosen(chosen, n_dp, n_v):
-    count = Gather.count(n_dp, n_v)
-    return pl.pallas_call(
-        functools.partial(chosen_kernel, n_dp, n_v),
-        out_shape=jax.ShapeDtypeStruct((n_dp,) + chosen.shape, chosen.dtype),
-        in_specs=[pl.BlockSpec(memory_space=pltpu.VMEM)],
-        out_specs=pl.BlockSpec(memory_space=pltpu.VMEM),
-        scratch_shapes=[pltpu.SemaphoreType.DMA((count,)), pltpu.SemaphoreType.DMA((count,))],
-        compiler_params=pltpu.CompilerParams(collective_id=1, has_side_effects=True),
-    )(chosen)
-
-
-def d_chosen_kernel(n_dp, n_v, in_ref, out_ref, bc, by, bx, bz, pc, py, px, ss, rs):
-    f32, bf = jnp.float32, jnp.bfloat16
-    p = Place(n_dp, n_v)
-    p.barrier()
-    q = Copies(p.me, ss, rs)
-    A, Y = p.A, p.Y
-    q.send(0, in_ref.at[:, :, :, 1 - p.c], bc, p.cp)
-    q.arrived(0, bc)
-    pc[...] = (in_ref[:, :, :, p.c].astype(f32) + bc[...].astype(f32)).astype(bf)
-    n = 1
+    n = gather.end
+    rows_v, total_m = ch_ref.shape[1], n_dp * MLM_PAD
+    chosen = al[...].reshape(total_m, D)
+    logits[...] = dot(table_ref[...], chosen, NT)
+    rows = table_ref.shape[0]
+    row_ids = (p.d * n_v + p.v) * rows + lax.broadcasted_iota(jnp.int32, (rows, 1), 0)
+    hits = row_ids == label_ref[...]
+    top = jnp.max(logits[...], axis=0, keepdims=True)
+    stats = (
+        top,
+        jnp.sum(jnp.exp(logits[...] - top), axis=0, keepdims=True),
+        jnp.sum(jnp.where(hits, logits[...], 0.0), axis=0, keepdims=True),
+    )
+    tall = total_m // 128
+    for k, values in enumerate(stats):
+        for r in range(tall):
+            st[k * tall + r : k * tall + r + 1, :] = values[:, r * 128 : (r + 1) * 128]
+
+    def merged(ref, amount):
+        tops = [ref[k, :tall, :] for k in range(amount)]
+        best = functools.reduce(jnp.maximum, tops)
+        parts = [ref[k, tall : 2 * tall, :] * jnp.exp(tops[k] - best) for k in range(amount)]
+        return best, sum(parts[1:], parts[0]), sum(ref[k, 2 * tall :, :] for k in range(amount))
+
+    sd[p.d] = st[...]
+    for k in range(1, n_dp):
+        q.send(n + k - 1, st, sd.at[p.d], others[k - 1])
+    for k in range(1, n_dp):
+        q.arrived(n + k - 1, sd.at[lax.rem(p.d + n_dp - k, n_dp)])
+    n = n + n_dp - 1
+    for k, values in enumerate(merged(sd, n_dp)):
+        sv[p.v, k * tall : (k + 1) * tall, :] = values
+    for k in range(1, n_v):
+        q.send(n + k - 1, sv.at[p.v], sv.at[p.v], partners[k - 1])
+    for k in range(1, n_v):
+        q.arrived(n + k - 1, sv.at[lax.rem(p.v + n_v - k, n_v)])
+    n = n + n_v - 1
+    best, total, target = merged(sv, n_v)
+    lse = best + jnp.log(total)
+    lse_s[...] = lse
+    lost = jnp.sum(jnp.where(tags_ref[...] >= 0, lse - target, 0.0), axis=1, keepdims=True)
+    lost = jnp.sum(lost, axis=0, keepdims=True) / count
+    loss_ref[...] = jnp.broadcast_to(lost, loss_ref.shape)
+    lse_row = jnp.concatenate([lse_s[r : r + 1, :] for r in range(tall)], axis=1)
+    d_log = (jnp.exp(logits[...] - lse_row) - hits.astype(f32)) * (1.0 / count)
+    dlog[...] = d_log.astype(bf)
+    made = dot(dlog[...], table_ref[...], TN).astype(bf)
+    part[...] = made.reshape(A, 2, Y, 2, rows_v, D)
+    q.send(n, part.at[:, :, :, 1 - p.c], bc, p.cp)
+    dtab_ref[...] = dot(dlog[...], chosen)
+    q.arrived(n, bc)
+    pc[...] = (part[:, :, :, p.c].astype(f32) + bc[...].astype(f32)).astype(bf)
+    n = n + 1
     for k in range(1, Y):
         q.send(n + k - 1, pc.at[:, :, lax.rem(p.y + k, Y)], by.at[k - 1], p.yp(k))
     total = pc[:, :, p.y].astype(f32)
@@ -319,43 +371,166 @@
         total = total + bz[k - 1].astype(f32)
     n = n + A - 1
     out_ref[p.v] = total.astype(bf)
-    for k in range(1, Y):
-        q.send(n + k - 1, out_ref.at[p.v], out_ref.at[p.v], p.yp(k))
-    q.send(n + Y - 1, out_ref.at[p.v], out_ref.at[p.v], p.cp)
-    for j in range(1, Y):
-        v = p.from_y(j) * 2 + p.c
-        q.arrived(n + j - 1, out_ref.at[v])
-        q.send(n + Y - 1 + j, out_ref.at[v], out_ref.at[v], p.cp)
-    for j in range(Y):
-        v = p.from_y(j) * 2 + 1 - p.c
-        q.arrived(n + Y - 1 + j, out_ref.at[v])
+    for k in range(1, n_v):
+        q.send(n + k - 1, out_ref.at[p.v], out_ref.at[p.v], partners[k - 1])
+    for k in range(1, n_v):
+        q.arrived(n + k - 1, out_ref.at[lax.rem(p.v + n_v - k, n_v)])
     q.finish()
 
 
-def reduce_d_chosen(partial, n_dp, n_v):
-    A, _, Y, _, rows, width = partial.shape
-    count = 1 + (Y - 1) + 1 + (A - 1) + (Y - 1) + Y
-    kind = partial.dtype
+def run_head(chosen, table, labels, n_dp, n_v):
+    f32, kind = jnp.float32, chosen.dtype
+    A, Y = n_dp // 2, n_v // 2
+    _, rows_v, width = chosen.shape
+    rows, total_m = table.shape[0], n_dp * MLM_PAD
+    tall = total_m // 128
+    count = Gather.count(n_dp, n_v) + n_dp - 1 + n_v - 1 + 1 + Y - 1 + 1 + A - 1 + n_v - 1
+    vmem = pl.BlockSpec(memory_space=pltpu.VMEM)
     return pl.pallas_call(
-        functools.partial(d_chosen_kernel, n_dp, n_v),
-        out_shape=jax.ShapeDtypeStruct((n_v, rows, width), kind),
-        in_specs=[pl.BlockSpec(memory_space=pltpu.VMEM)],
-        out_specs=pl.BlockSpec(memory_space=pltpu.VMEM),
+        functools.partial(head_kernel, n_dp, n_v),
+        out_shape=[
+            jax.ShapeDtypeStruct(chosen.shape, kind),
+            jax.ShapeDtypeStruct(table.shape, f32),
+            jax.ShapeDtypeStruct((8, 128), f32),
+        ],
+        in_specs=[vmem] * 4,
+        out_specs=[vmem] * 3,
         scratch_shapes=[
-            pltpu.VMEM((A, 2, Y, rows, width), kind),
-            pltpu.VMEM((Y - 1, A, 2, rows, width), kind),
-            pltpu.VMEM((A, rows, width), kind),
-            pltpu.VMEM((A - 1, rows, width), kind),
-            pltpu.VMEM((A, 2, Y, rows, width), kind),
-            pltpu.VMEM((A, 2, rows, width), kind),
-            pltpu.VMEM((A, rows, width), kind),
+            pltpu.VMEM((n_dp,) + chosen.shape, kind),
+            pltpu.VMEM((rows, total_m), f32),
+            pltpu.VMEM((rows, total_m), kind),
+            pltpu.VMEM((3 * tall, 128), f32),
+            pltpu.VMEM((n_dp, 3 * tall, 128), f32),
+            pltpu.VMEM((n_v, 3 * tall, 128), f32),
+            pltpu.VMEM((tall, 128), f32),
+            pltpu.VMEM((A, 2, Y, 2, rows_v, width), kind),
+            pltpu.VMEM((A, 2, Y, rows_v, width), kind),
+            pltpu.VMEM((Y - 1, A, 2, rows_v, width), kind),
+            pltpu.VMEM((A, rows_v, width), kind),
+            pltpu.VMEM((A - 1, rows_v, width), kind),
+            pltpu.VMEM((A, 2, Y, rows_v, width), kind),
+            pltpu.VMEM((A, 2, rows_v, width), kind),
+            pltpu.VMEM((A, rows_v, width), kind),
             pltpu.SemaphoreType.DMA((count,)),
             pltpu.SemaphoreType.DMA((count,)),
         ],
         compiler_params=pltpu.CompilerParams(
             collective_id=2, has_side_effects=True, vmem_limit_bytes=56 << 20
         ),
-    )(partial)
+    )(chosen, table, labels.reshape(1, total_m), labels.reshape(tall, 128))
+
+
+def norm_kernel(n_dp, n_v, layer_ref, small_ref, table_ref, out_ref, sd, sv, ss, rs):
+    f32 = jnp.float32
+    d, v = lax.axis_index("dp"), lax.axis_index("vocab")
+    others = [(lax.rem(d + k, n_dp), v) for k in range(1, n_dp)]
+    partners = [(d, lax.rem(v + k, n_v)) for k in range(1, n_v)]
+    sem = pltpu.get_barrier_semaphore()
+    for partner in others + partners:
+        pl.semaphore_signal(sem, 1, device_id=partner, device_id_type=MESH)
+
+    def square(values):
+        values = values.astype(f32)
+        values = values * values
+        while values.ndim > 2:
+            values = jnp.sum(values, axis=0)
+        return jnp.sum(jnp.sum(values, axis=0, keepdims=True), axis=1, keepdims=True)
+
+    total = square(table_ref[...])
+    total = total + jnp.where(v == 0, square(layer_ref[...]), 0.0)
+    total = total + jnp.where((v == 0) & (d == 0), square(small_ref[...]), 0.0)
+    sd[d] = jnp.broadcast_to(total, sd.shape[1:])
+    pl.semaphore_wait(sem, n_dp - 1 + n_v - 1)
+    q = Copies((d, v), ss, rs)
+    for k in range(1, n_dp):
+        q.send(k - 1, sd.at[d], sd.at[d], others[k - 1])
+    for k in range(1, n_dp):
+        q.arrived(k - 1, sd.at[lax.rem(d + n_dp - k, n_dp)])
+    sv[v] = jnp.sum(sd[...], axis=0)
+    for k in range(1, n_v):
+        q.send(n_dp + k - 2, sv.at[v], sv.at[v], partners[k - 1])
+    for k in range(1, n_v):
+        q.arrived(n_dp + k - 2, sv.at[lax.rem(v + n_v - k, n_v)])
+    out_ref[...] = jnp.sum(sv[...], axis=0)
+    q.finish()
+
+
+def run_norm(layer, small, table, n_dp, n_v):
+    f32 = jnp.float32
+    vmem = pl.BlockSpec(memory_space=pltpu.VMEM)
+    count = n_dp + n_v - 2
+    return pl.pallas_call(
+        functools.partial(norm_kernel, n_dp, n_v),
+        out_shape=jax.ShapeDtypeStruct((8, 128), f32),
+        in_specs=[vmem] * 3,
+        out_specs=vmem,
+        scratch_shapes=[
+            pltpu.VMEM((n_dp, 8, 128), f32),
+            pltpu.VMEM((n_v, 8, 128), f32),
+            pltpu.SemaphoreType.DMA((count,)),
+            pltpu.SemaphoreType.DMA((count,)),
+        ],
+        compiler_params=pltpu.CompilerParams(
+            collective_id=4, has_side_effects=True, vmem_limit_bytes=40 << 20
+        ),
+    )(layer, small, table)
+
+
+def adam_kernel(rates, scal_ref, *refs):
+    n = len(rates)
+    grads, ins, outs = refs[:n], refs[n : 4 * n], refs[4 * n : 7 * n]
+    bufs, sem_i, sem_o = refs[7 * n : 10 * n], refs[10 * n], refs[10 * n + 1]
+    loads = [pltpu.make_async_copy(ins[k], bufs[k], sem_i.at[k]) for k in range(3 * n)]
+    for copy in loads:
+        copy.start()
+    coef, one_hat, two_hat = scal_ref[0], scal_ref[1], scal_ref[2]
+    stores = []
+    for i, rate in enumerate(rates):
+        master, first, second = bufs[3 * i : 3 * i + 3]
+        for copy in loads[3 * i : 3 * i + 3]:
+            copy.wait()
+        rows = master.shape[0]
+        chunk = 32 if rows % 32 == 0 else rows
+
+        def update(c, _, i=i, rate=rate, master=master, first=first, second=second, chunk=chunk):
+            at = pl.ds(c * chunk if isinstance(c, int) else pl.multiple_of(c * chunk, chunk), chunk)
+            g = grads[i][at, :].astype(jnp.float32) * coef
+            one = BETA_ONE * first[at, :] + (1.0 - BETA_ONE) * g
+            two = BETA_TWO * second[at, :] + (1.0 - BETA_TWO) * g * g
+            old = master[at, :]
+            move = one * one_hat / (jnp.sqrt(two * two_hat) + ADAM_EPS) + DECAY * old
+            first[at, :] = one
+            second[at, :] = two
+            master[at, :] = old - rate * move
+            return 0
+
+        if rows == chunk:
+            update(0, 0)
+        else:
+            lax.fori_loop(0, rows // chunk, update, 0)
+        for k in range(3 * i, 3 * i + 3):
+            copy = pltpu.make_async_copy(bufs[k], outs[k], sem_o.at[k])
+            copy.start()
+            stores.append(copy)
+    for copy in stores:
+        copy.wait()
+
+
+def run_adam(scalars, grads, states, rates):
+    hbm = pl.BlockSpec(memory_space=pl.ANY)
+    n = len(rates)
+    flat = [array for state in states for array in state]
+    return pl.pallas_call(
+        functools.partial(adam_kernel, rates),
+        out_shape=[jax.ShapeDtypeStruct(a.shape, a.dtype) for a in flat],
+        in_specs=[pl.BlockSpec(memory_space=pltpu.SMEM)]
+        + [pl.BlockSpec(memory_space=pltpu.VMEM)] * n
+        + [hbm] * (3 * n),
+        out_specs=[hbm] * (3 * n),
+        scratch_shapes=[pltpu.VMEM(a.shape, a.dtype) for a in flat]
+        + [pltpu.SemaphoreType.DMA((3 * n,)), pltpu.SemaphoreType.DMA((3 * n,))],
+        compiler_params=pltpu.CompilerParams(vmem_limit_bytes=56 << 20),
+    )(scalars, *grads, *flat)
 
 
 def grads_kernel(n_dp, n_v, g_ref, e_ref, t_ref, g_out, e_out, t_out, bx, px, bz, ebx, epx, ebz, ss, rs, ls):
@@ -864,7 +1039,6 @@
     n_v = lax.axis_size("vocab")
     d_idx = lax.axis_index("dp")
     v_idx = lax.axis_index("vocab")
-    count = n_dp * MLM
     own_rows = embed_master.shape[0]
     tokens_n = SEGS * SEG
     rb = qkv_master.shape[1]
@@ -892,9 +1066,12 @@
             full[8:].reshape(1, 4 * rb, D),
         )
 
-    ids_all = lax.all_gather(ids, "dp", axis=0, tiled=True)
-    labels = jnp.full((n_dp, MLM_PAD - MLM), -1, jnp.int32)
-    labels_all = jnp.concatenate([lax.all_gather(mlm_label, "dp", axis=0, tiled=True), labels], axis=1)
+    ints = jnp.concatenate([ids[0], mlm_label[0]])[None]
+    ints = jnp.pad(ints, ((0, 0), (0, ceil_to(ints.shape[1], 128) - ints.shape[1])), constant_values=-1)
+    ints_all = gather_ints(ints, n_dp)[:, 0]
+    ids_all = ints_all[:, :tokens_n]
+    labels_all = ints_all[:, tokens_n : tokens_n + MLM]
+    labels_all = jnp.pad(labels_all, ((0, 0), (0, MLM_PAD - MLM)), constant_values=-1)
     holder = ids_all // own_rows
     local_row = ids_all % own_rows
     order = jnp.arange(tokens_n, dtype=jnp.int32)
@@ -947,29 +1124,9 @@
     at_rows = jnp.concatenate([at_rows, jnp.full((MLM_PAD - MLM,), -1, jnp.int32)])
     *saved, chosen = run_forward(w_all, tokens, marks, resets[0], vec, extras_master, at_rows)
     rows_v = MLM_PAD // n_v
-    chosen_all = gather_chosen(chosen.reshape(n_v, rows_v, D), n_dp, n_v).reshape(n_dp * MLM_PAD, D)
-
-    logits = jnp.einsum("md,vd->mv", chosen_all, table, preferred_element_type=f32)
-    row_ids = (d_idx * n_v + v_idx) * own_rows + own_slots
-    label_flat = labels_all.reshape(n_dp * MLM_PAD)
-    hits = label_flat[:, None] == row_ids[None, :]
-    top = lax.pmax(jnp.max(logits, axis=-1), ("dp", "vocab"))
-    sums, target = lax.psum(
-        (
-            jnp.sum(jnp.exp(logits - top[:, None]), axis=-1),
-            jnp.sum(jnp.where(hits, logits, 0.0), axis=-1),
-        ),
-        ("dp", "vocab"),
-    )
-    lse = top + jnp.log(sums)
-    real = label_flat >= 0
-    loss = jnp.sum(jnp.where(real, lse - target, 0.0)) / count
-    d_logits = ((jnp.exp(logits - lse[:, None]) - hits.astype(f32)) / count).astype(bf)
-    d_table = jnp.einsum("mv,md->vd", d_logits, chosen_all, preferred_element_type=f32)
-    d_part = jnp.dot(d_logits, table, preferred_element_type=f32).astype(bf)
-    d_chosen = reduce_d_chosen(
-        d_part.reshape(n_dp // 2, 2, n_v // 2, 2, rows_v, D), n_dp, n_v
-    ).reshape(MLM_PAD, D)
+    d_chosen, d_table, loss = run_head(chosen.reshape(n_v, rows_v, D), table, labels_all, n_dp, n_v)
+    loss = loss[0, 0]
+    d_chosen = d_chosen.reshape(MLM_PAD, D)
     small_rows = EXT + 12
     e_rows = ceil_to(-(-small_rows // (n_dp * n_v)), 16)
     at = jnp.arange(n_dp * cap, dtype=jnp.int32)
@@ -1003,34 +1160,40 @@
     def whole_d_table(_):
         d_all = d_tok.reshape(SEGS, ROWS, D)[:, MEM : MEM + SEG].reshape(tokens_n, D)
         d_all = lax.all_gather(d_all, "dp", axis=0, tiled=True)
+        row_ids = (d_idx * n_v + v_idx) * own_rows + own_slots
         onehot = (ids_all.reshape(-1)[:, None] == row_ids[None, :]).astype(bf)
         return jnp.einsum("tv,td->vd", onehot, d_all, preferred_element_type=f32)
 
     s_table = d_table + lax.cond(overflow, whole_d_table, packed_d_table, 0)
-    s_qkv, s_out, s_up, s_down = from_blocks(g_blocks.astype(f32))
-    small_all = small_all.astype(f32).reshape(n_dp * n_v * e_rows, D)
-    g_ext = small_all[: extras_master.shape[0]]
-    g_vec = small_all[EXT:small_rows]
+    small_all = small_all.reshape(n_dp * n_v * e_rows, D)
+    norm = jnp.sqrt(run_norm(g_blocks, small_all[:small_rows], s_table, n_dp, n_v)[0, 0])
+    s_qkv, s_out, s_up, s_down = (grad[0] for grad in from_blocks(g_blocks))
+    g_ext = small_all[:EXT].astype(f32)
+    g_vec = small_all[EXT:small_rows].astype(f32)
     g_up_bias = g_vec[5:9].reshape(4, n_dp, rb).transpose(1, 0, 2).reshape(4, D)
-    g_vec = jnp.concatenate([g_vec[:5], g_up_bias, g_vec[9:]]).reshape(vectors_master.shape)
-
-    layer_sq = jnp.where(v_idx == 0, squares((s_qkv, s_out, s_up, s_down)), 0.0)
-    small_sq = jnp.where((v_idx == 0) & (d_idx == 0), squares((g_vec, g_ext)), 0.0)
-    norm = jnp.sqrt(lax.psum(layer_sq + squares((s_table,)) + small_sq, ("dp", "vocab")))
+    g_vec = jnp.concatenate([g_vec[:5], g_up_bias, g_vec[9:]])
     coef = jnp.minimum(1.0, CLIP / (norm + 1e-06))
-    step_count = step[0].astype(f32)
-    results = [loss, norm]
-    for master, first, second, grad, rate in (
-        (qkv_master, qkv_first, qkv_second, s_qkv, LR_BIG),
-        (out_master, out_first, out_second, s_out, LR_BIG),
-        (up_master, up_first, up_second, s_up, LR_BIG),
-        (down_master, down_first, down_second, s_down, LR_BIG),
-        (embed_master, embed_first, embed_second, s_table, LR_BIG),
-        (vectors_master, vectors_first, vectors_second, g_vec, LR_SMALL),
-        (extras_master, extras_first, extras_second, g_ext, LR_SMALL),
-    ):
-        results.extend(adam(master, first, second, grad, coef, step_count, rate))
-    return tuple(results)
+    t = step[0].astype(f32)
+    scalars = jnp.stack([coef, 1.0 / (1.0 - BETA_ONE**t), 1.0 / (1.0 - BETA_TWO**t)])
+    wide = (12, D)
+    states = (
+        (embed_master, embed_first, embed_second),
+        (qkv_master[0], qkv_first[0], qkv_second[0]),
+        (out_master[0], out_first[0], out_second[0]),
+        (up_master[0], up_first[0], up_second[0]),
+        (down_master[0], down_first[0], down_second[0]),
+        (extras_master, extras_first, extras_second),
+        (vectors_master.reshape(wide), vectors_first.reshape(wide), vectors_second.reshape(wide)),
+    )
+    new = run_adam(
+        scalars,
+        (s_table, s_qkv, s_out, s_up, s_down, g_ext, g_vec),
+        states,
+        (LR_BIG, LR_BIG, LR_BIG, LR_BIG, LR_BIG, LR_SMALL, LR_SMALL),
+    )
+    layer = [value[None] for value in new[3:15]]
+    vectors = [value.reshape(vectors_master.shape) for value in new[18:]]
+    return (loss, norm, *layer, *new[:3], *vectors, *new[15:18])
 
 
 def solution(mesh):

time: 614 us -> 450 us (0.73)
  blocking collectives: 168 us -> 0 us
  Pallas kernels: 320 us -> 364 us
  other arithmetic: 40.8 us -> 18 us
  matrix products: 17.6 us -> 5.76 us
  between operations: 25.1 us -> 18.9 us
    psum x2 -> x0, blocking collectives: 75.9 us -> none  [per_device(): lax.psum((jnp.sum(jnp.exp(logits - top[:, None]), axis=-1), jnp.sum(jnp.w...]
    all_gather x2 -> x0, blocking collectives: 51.8 us -> none  [the longest x1 32.4 us: per_device(): ids_all = lax.all_gather(ids, 'dp', axis=0, tiled=True)]
    pmax x1 -> x0, blocking collectives: 40.4 us -> none  [per_device(): top = lax.pmax(jnp.max(logits, axis=-1), ('dp', 'vocab'))]
    pallas_call x2 -> x4, Pallas kernels: 56.3 us -> 96.7 us  [the longest x1 60.6 us: run_head(): pl.pallas_call(functools.partial(head_kernel, n_dp, n_v), out_shape=[jax....]
    sub x7 -> x0, other arithmetic: 20.3 us -> none  [adam(): master - rate * (first_hat / (jnp.sqrt(second_hat) + ADAM_EPS) + DECAY *...]
    mul x5 -> x0, local copies, waits for them, and re-layouts: 11.3 us -> none  [adam(): clipped = grad * coef]
    dot_general x3 -> x0, matrix products: 9.66 us -> none  [the longest x1 4.94 us: per_device(): jnp.einsum('mv,md->vd', d_logits, chosen_all, preferred_element_type=f32)]
    pallas_call x1, Pallas kernels: 98.7 us -> 105 us  [gather_weights(): pl.pallas_call(functools.partial(weights_kernel, n_dp, n_v), out_shape=(j...]
where the time goes in v2:
time: 450 us; the launch traced here: 442 us
  Pallas kernels  364 us (81%)
  local copies, waits for them, and re-layouts  26.8 us (6%)
  between operations  18.9 us (4%)
  other arithmetic  18 us (4%)
  loops' own time  9.11 us (2%)
  matrix products  5.76 us (1%)
    pallas_call x1, Pallas kernels, gather_weights(): pl.pallas_call(functools.partial(weights_kernel, n_dp, n_v), out_shape=(j...  105 us
    pallas_call x1, Pallas kernels, reduce_grads(): pl.pallas_call(functools.partial(grads_kernel, n_dp, n_v), out_shape=(jax...  82.7 us
    pallas_call x1, Pallas kernels, run_head(): pl.pallas_call(functools.partial(head_kernel, n_dp, n_v), out_shape=[jax....  60.6 us
    pallas_call x1, Pallas kernels, run_backward(): pl.pallas_call(functools.partial(backward_kernel, cuts), out_shape=[jax.S...  45 us
    pallas_call x1, Pallas kernels, run_forward(): pl.pallas_call(forward_kernel, out_shape=[jax.ShapeDtypeStruct(s, k) for...  34.5 us
    pallas_call x1, Pallas kernels, run_adam(): pl.pallas_call(functools.partial(adam_kernel, rates), out_shape=[jax.Shap...  16.2 us
    pallas_call x1, Pallas kernels, run_norm(): pl.pallas_call(functools.partial(norm_kernel, n_dp, n_v), out_shape=jax.S...  10.2 us
    pallas_call x1, Pallas kernels, gather_ints(): pl.pallas_call(functools.partial(ints_kernel, n_dp), out_shape=jax.ShapeD...  9.7 us

profile of v2, /device:TPU:0, one launch (start us, length us, event | category | flops | bytes accessed | tf_op | source)
XLA Modules:
  0.0 442.3 jit_solution(18218797192056548723)
XLA Ops:
  7.2 1.4 convert_element_type.57
  11.2 1.4 pad_maximum_fusion.w_ref
  14.5 9.7 %shard_map.434 = s32[8,1,896]{2,1,0:T(1,128)} custom-call(s32[1,896]{1,0:T(1,128)} %pad.24.in_ref), custom_call_target="tpu_custom_call" | custom-call | tf_op jit(solution)/shard_map/pallas_call | solution.py:268
  25.2 4.4 convert_reduce_fusion
  30.1 1.3 convolution_convert_fusion
  31.5 104.8 %shard_map.435 = (bf16[8,12,96,768]{3,2,1,0:T(8,128)(2,1)}, bf16[8,4,48,768]{3,2,1,0:T(8,128)(2,1)}) custom-call(bf16[12,96,768]{2,1,0:T(8,128)(2,1)} %pad_maximum_fusion.w_ref, bf16[8,48,768]{2,1,0:T(8,128)(2,1)} %bitcast.137), custom_call_target="tpu_custom_call" | custom-call | tf_op jit(solution)/shard_map/pallas_call | solution.py:234
  137.9 12.7 %conditional.2 = (bf16[768,768]{1,0:T(8,128)(2,1)S(1)}) conditional(s32[]{:T(128)} %convert_element_type.61, (s32[2,384]{1,0:T(2,128)S(1)}, bf16[8,4,48,768]{3,2,1,0:T(8,128)(2,1)}) %tuple.20, (s32[1,728]{1,0:T(1,128)S(1)}, s32[]{:T(128)}, bf16[480,768]{1,0:T(8,128)(2,1)S(1)}) %tuple.42), branch_computations={%region_3.4_spmd, %region_4.6_spmd} | conditional | flops 4297893888 | bytes 41179808 | solution.py:1117
  137.9 3.8 fusion.2
  154.5 34.5 %shard_map.436 = (f32[2,384,768]{2,1,0:T(8,128)}, bf16[2,768,768]{2,1,0:T(8,128)(2,1)}, bf16[3,768,768]{2,1,0:T(8,128)(2,1)}, bf16[2,12,384,384]{3,2,1,0:T(8,128...) custom-call(bf16[8,12,96,768]{3,2,1,0:T(8,128)(2,1)} %get-tuple-elem, ...), custom_call_target="tpu_custom_call" | custom-call | tf_op jit(solution)/shard_map/pallas_call | solution.py:792
  189.7 60.6 %shard_map.437 = (bf16[4,32,768]{2,1,0:T(8,128)(2,1)}, f32[480,768]{1,0:T(8,128)}, f32[8,128]{1,0:T(8,128)}) custom-call(bf16[4,32,768]{2,1,0:T(8,128)(2,1)} %bitcast.144, bf16[480,768]{1,0:T(8,128)(2,1)S(1)} %copy-done.4, s32[1,1024]{1,0:T(1,128)} %bitcast.150, s32[8,128]{1,0:T(8,128)} %pad.27.tags_ref), custom_call_target="tpu_custom_call" | custom-call | tf_op jit(solution)/shard_map/pallas_call | solution.py:389
  250.3 1.2 slice.68
  252.8 45.0 %shard_map.438 = (bf16[3,768,768]{2,1,0:T(8,128)(2,1)}, f32[424,768]{1,0:T(8,128)}, bf16[384,768]{1,0:T(8,128)(2,1)}, bf16[768,768]{1,0:T(8,128)(2,1)}) custom-call(bf16[8,12,96,768]{3,2,1,0:T(8,128)(2,1)} %get-tuple-element.108.w_hbm, f32[2,384,768]{2,1,0:T(8,128)} %get-tuple-element.112.x_i, bf16[2,768,768]{2,1,0:T(8,128)(2,1)} %get-tuple-element.113.hc_i, ...), custom_call_target="tpu_custom_call" | custom-call | tf_op jit(solution)/shard_map/pallas_call | solution.py:970
  297.8 1.4 convert_element_type.62
  300.0 82.7 %shard_map.439 = (bf16[12,96,768]{2,1,0:T(8,128)(2,1)}, bf16[8,4,16,768]{3,2,1,0:T(8,128)(2,1)}, bf16[8,48,768]{2,1,0:T(8,128)(2,1)S(1)}) custom-call(bf16[3,4,2,96,768]{4,3,2,1,0:T(8,128)(2,1)} %bitcast.114, bf16[4,2,16,768]{3,2,1,0:T(8,128)(2,1)} %dynamic-slice_bitcast_fusion.e_ref, bf16[8,48,768]{2,1,0:T(8,128)(2,1)} %bitcast.136), custom_call_target="tpu_custom_call" | custom-call | tf_op jit(solution)/shard_map/pallas_call | solution.py:619
  382.7 2.0 slice.83.small_ref
  385.7 1.7 add.174.table_ref.refs_0_
  387.7 10.2 %shard_map.440 = f32[8,128]{1,0:T(8,128)S(1)} custom-call(bf16[12,96,768]{2,1,0:T(8,128)(2,1)S(1)} %copy-done.1, bf16[418,768]{1,0:T(8,128)(2,1)S(1)} %copy-done.2, f32[480,768]{1,0:T(8,128)S(1)} %add.174.table_ref.refs_0_), custom_call_target="tpu_custom_call" | custom-call | tf_op jit(solution)/shard_map/pallas_call | solution.py:462
  403.8 1.0 copy.104
  404.9 1.9 squeeze_reshape.10.refs_3_
  406.8 1.1 slice_convert_fusion.refs_5_
  413.3 16.2 %shard_map.441 = (f32[480,768]{1,0:T(8,128)}, f32[480,768]{1,0:T(8,128)}, f32[480,768]{1,0:T(8,128)}, f32[96,2304]{1,0:T(8,128)}, f32[96,2304]{1,0:T(8,128)}, /*...) custom-call(f32[3]{0:T(128)} %pad_maximum_fusion.3.scal_ref, ...), custom_call_target="tpu_custom_call" | custom-call | tf_op jit(solution)/shard_map/pallas_call | solution.py:523
  429.5 1.5 copy.96
  431.0 1.5 copy.97
  432.5 1.5 copy.98
  (107 shorter events, 24.4 us)
Async XLA Ops:
  7.2 1.6 copy-start.7
  9.7 1.0 copy-start.10
  9.7 1.3 copy-start.8
  11.2 1.9 copy-start.6
  13.1 0.7 copy-start.14
  13.1 0.7 copy-start.16
  13.2 124.7 %copy-start.3 = (bf16[480,768]{1,0:T(8,128)(2,1)}, bf16[480,768]{1,0:T(8,128)(2,1)S(1)}, u32[]{:S(2)}) copy-start(bf16[480,768]{1,0:T(8,128)(2,1)S(1)} %convert_element_type.59.table_ref) | copy-start | bytes 2211844
  30.1 107.5 %copy-start.15 = (s32[1,728]{1,0:T(1,128)S(1)}, s32[1,728]{1,0:T(1,128)}, u32[]{:S(2)}) copy-start(s32[1,728]{1,0:T(1,128)} %param.32) | copy-start | bytes 8740
  137.9 14.9 %copy-start.11 = (f32[1,9216]{1,0:T(1,128)S(1)}, f32[1,9216]{1,0:T(1,128)}, u32[]{:S(2)}) copy-start(f32[1,9216]{1,0:T(1,128)} %param.52) | copy-start | bytes 110596
  137.9 15.8 %copy-start.17 = (s32[1,112]{1,0:T(1,128)S(1)}, s32[1,112]{1,0:T(1,128)}, u32[]{:S(2)}) copy-start(s32[1,112]{1,0:T(1,128)} %param.34) | copy-start | bytes 1348
  154.5 35.2 %copy-start.4 = (bf16[480,768]{1,0:T(8,128)(2,1)S(1)}, bf16[480,768]{1,0:T(8,128)(2,1)}, u32[]{:S(2)}) copy-start(bf16[480,768]{1,0:T(8,128)(2,1)} %copy-done.3) | copy-start | bytes 2211844
  385.6 1.9 copy-start.1
  385.7 2.1 copy-start.2
  387.7 10.2 %copy-start = (f32[480,768]{1,0:T(8,128)}, f32[480,768]{1,0:T(8,128)S(1)}, u32[]{:S(2)}) copy-start(f32[480,768]{1,0:T(8,128)S(1)} %add.174.table_ref.refs_0_) | copy-start | bytes 4423684
  403.8 2.9 copy-start.9
  404.9 5.8 %copy-start.12 = (f32[1,9216]{1,0:T(1,128)S(1)}, f32[1,9216]{1,0:T(1,128)}, u32[]{:S(2)}) copy-start(f32[1,9216]{1,0:T(1,128)} %param.53) | copy-start | bytes 110596
  404.9 7.1 %copy-start.13 = (f32[1,9216]{1,0:T(1,128)S(1)}, f32[1,9216]{1,0:T(1,128)}, u32[]{:S(2)}) copy-start(f32[1,9216]{1,0:T(1,128)} %param.54) | copy-start | bytes 110596

commit v3 on v2

--- a/solution.py
+++ b/solution.py
@@ -91,7 +91,8 @@
 
 
 class Gather:
-    def __init__(self, place, copies, base, ref, own=None, shared=False):
+    def __init__(self, place, copies, base, ref, own=None, shared=False, flat=False):
+        self.flat = flat
         self.p, self.q, self.base, self.ref, self.own = place, copies, base, ref, own
         self.least = 1 if shared else 0
         A, Y = place.A, place.Y
@@ -119,8 +120,9 @@
             self.q.send(self.x0 + slot, src, self.at(slot), p.xp)
         if slot < self.least:
             return
-        for k in range(1, p.Y):
-            self.q.send(self.y0 + slot * (p.Y - 1) + k - 1, src, self.at(slot), p.yp(k))
+        if not self.flat:
+            for k in range(1, p.Y):
+                self.q.send(self.y0 + slot * (p.Y - 1) + k - 1, src, self.at(slot), p.yp(k))
         self.q.send(self.c0 + slot * p.Y, src, self.at(slot), p.cp)
 
     def start(self):
@@ -143,6 +145,8 @@
 
     def step_y(self):
         p = self.p
+        if self.flat:
+            return
         for slot in range(self.least, 2 * p.A):
             for j in range(1, p.Y):
                 self.q.arrived(self.y0 + slot * (p.Y - 1) + j - 1, self.at(slot, j))
@@ -151,128 +155,169 @@
     def step_c(self):
         p = self.p
         for slot in range(self.least, 2 * p.A):
-            for j in range(p.Y):
+            for j in range(1 if self.flat else p.Y):
                 self.q.arrived(self.c0 + slot * p.Y + j, self.at(slot, j, 1 - p.c))
 
 
-def weights_kernel(n_dp, n_v, w_ref, tok_ref, out_ref, tok_out, ss, rs, ls):
+def front_kernel(
+    n_dp, n_v, cap, w_ref, table_ref, ints_ref,
+    out_ref, tok_out, ints_out, pick_out, slot_out, rank_out,
+    packed, hold, upper, ss, rs, ls,
+):
+    f32, bf = jnp.float32, jnp.bfloat16
     p = Place(n_dp, n_v)
-    others = []
-    for k in range(1, p.A):
-        others.append((p.to_a(k) * 2 + 1 - p.x, p.v))
-    p.barrier(others)
     q = Copies(p.me, ss, rs)
-    groups = w_ref.shape[0] // n_v
-    local = pltpu.make_async_copy(tok_ref.at[p.d], tok_out.at[p.d, p.v], ls.at[0])
-    local.start()
-    locals_ = [local]
+    others = [(lax.rem(p.d + k, n_dp), p.v) for k in range(1, n_dp)]
+    partners = [(p.d, lax.rem(p.v + k, n_v)) for k in range(1, n_v)]
+    sem = pltpu.get_barrier_semaphore()
+    for partner in others + partners:
+        pl.semaphore_signal(sem, 1, device_id=partner, device_id_type=MESH)
+    own = pltpu.make_async_copy(w_ref, out_ref.at[p.d], ls.at[0])
+    own.start()
+    ints_out[p.d] = ints_ref[...]
+    pl.semaphore_wait(sem, n_dp - 1 + n_v - 1)
+    base = 0
+    for k in range(1, n_dp):
+        q.send(base + k - 1, ints_ref, ints_out.at[p.d], others[k - 1])
+    i0 = base
+    base = base + n_dp - 1
     gathers = []
-    base = 0
-    own = pltpu.make_async_copy(w_ref, out_ref.at[p.d], ls.at[1])
-    own.start()
-    locals_.append(own)
-    for g in range(groups):
-        gather = Gather(
-            p,
-            q,
-            base,
-            lambda d, v, g=g: out_ref.at[d, g * n_v + v],
-            own=w_ref.at[g * n_v + p.v],
-            shared=True,
-        )
+    for g in range(3):
+        if g < 2:
+            gather = Gather(
+                p,
+                q,
+                base,
+                lambda d, v, g=g: out_ref.at[d, g * n_v + v],
+                own=w_ref.at[g * n_v + p.v],
+                shared=True,
+            )
+        else:
+            half = n_v // 2
+            gather = Gather(
+                p,
+                q,
+                base,
+                lambda d, v: out_ref.at[d, pl.ds(2 * n_v + (v % 2) * half, half)],
+                own=w_ref.at[pl.ds(2 * n_v + p.c * half, half)],
+                shared=True,
+                flat=True,
+            )
         base = gather.end
         gathers.append(gather)
+        gather.start()
+
+    tokens_n, wide = SEGS * SEG, ceil_to(SEGS * SEG, 128)
+    n_dev = n_dp * n_v
+    rows = table_ref.shape[0]
+    lane = lax.broadcasted_iota(jnp.int32, (1, wide), 1)
+    valid = lane < tokens_n
+    device = lax.broadcasted_iota(jnp.int32, (n_dev, 1), 0)
+    least = device * rows
+    upper[...] = (lax.broadcasted_iota(jnp.int32, (wide, 1), 0) < lane).astype(bf)
+    place = lax.broadcasted_iota(jnp.int32, (cap, 1), 0).astype(f32)
+    row_at = lax.broadcasted_iota(jnp.int32, (1, rows), 1).astype(f32) + 1.0
+    low = (p.d * n_v + p.v) * rows
+    for k in range(1, n_dp):
+        q.arrived(i0 + k - 1, ints_out.at[lax.rem(p.d + n_dp - k, n_dp)])
+    most = jnp.zeros((1, 1), f32)
+    batch = hold.shape[0] // n_dev
+    for start in range(0, n_dp, batch):
+        for i in range(batch):
+            ids = ints_out[start + i, :, :wide]
+            held = (ids >= least) & (ids < least + rows) & valid
+            hold[i * n_dev : (i + 1) * n_dev, :] = held.astype(f32).astype(bf)
+        before = dot(hold[...], upper[...])
+        for i in range(batch):
+            ids = ints_out[start + i, :, :wide]
+            held = hold[i * n_dev : (i + 1) * n_dev, :].astype(f32)
+            rank = jnp.sum(held * before[i * n_dev : (i + 1) * n_dev, :], axis=0, keepdims=True)
+            holder = jnp.sum(held * device.astype(f32), axis=0, keepdims=True)
+            most = jnp.maximum(most, jnp.max(rank, axis=1, keepdims=True))
+            slot_out[start + i : start + i + 1, :] = jnp.where(valid, holder * cap + rank, -1.0)
+            mine = (ids >= low) & (ids < low + rows) & valid
+            row = jnp.where(mine, (ids - low).astype(f32) + 1.0, 0.0)
+            taken = jnp.sum(jnp.where(rank == place, row, 0.0), axis=1, keepdims=True)
+            pick = (taken == row_at).astype(f32).astype(bf)
+            pick_out[(start + i) * cap : (start + i + 1) * cap, :] = pick
+    rank_out[...] = jnp.broadcast_to(most, rank_out.shape)
+    packed[...] = dot(pick_out[...], table_ref[...]).astype(bf).reshape(packed.shape)
+    first = base
     for k in range(1, n_dp):
         to = lax.rem(p.d + k, n_dp)
-        q.send(base + k - 1, tok_ref.at[to], tok_out.at[p.d, p.v], (to, p.v))
-    for gather in gathers:
-        gather.start()
-    local.wait()
-    first = base
+        q.send(first + k - 1, packed.at[to], tok_out.at[p.d, p.v], others[k - 1])
+    local = pltpu.make_async_copy(packed.at[p.d], tok_out.at[p.d, p.v], ls.at[1])
+    local.start()
     base = base + n_dp - 1
-
-    def relay(slot, src_d):
+    y0, c0 = base, base + n_dp * (p.Y - 1)
+
+    def relay(slot, src, src_d):
         for k in range(1, p.Y):
-            number = base + slot * (p.Y - 1) + k - 1
-            q.send(number, tok_out.at[src_d, p.v], tok_out.at[src_d, p.v], p.yp(k))
-        number = base + n_dp * (p.Y - 1) + slot * p.Y
-        q.send(number, tok_out.at[src_d, p.v], tok_out.at[src_d, p.v], p.cp)
-
-    relay(0, p.d)
+            q.send(y0 + slot * (p.Y - 1) + k - 1, src, tok_out.at[src_d, p.v], p.yp(k))
+        q.send(c0 + slot * p.Y, src, tok_out.at[src_d, p.v], p.cp)
+
+    relay(0, packed.at[p.d], p.d)
+    g0, g1, g2 = gathers
+    g0.step_a()
+    g0.step_x()
+    g1.step_a()
     for k in range(1, n_dp):
         src_d = lax.rem(p.d + n_dp - k, n_dp)
         q.arrived(first + k - 1, tok_out.at[src_d, p.v])
-        relay(k, src_d)
-    for gather in gathers:
-        gather.step_a()
-    for gather in gathers:
-        gather.step_x()
+        relay(k, tok_out.at[src_d, p.v], src_d)
+    g0.step_y()
+    g1.step_x()
+    g2.step_a()
+    g1.step_y()
     for slot in range(n_dp):
         src_d = lax.rem(p.d + n_dp - slot, n_dp)
         for j in range(1, p.Y):
-            v = p.from_y(j) * 2 + p.c
-            q.arrived(base + slot * (p.Y - 1) + j - 1, tok_out.at[src_d, v])
-            number = base + n_dp * (p.Y - 1) + slot * p.Y + j
-            q.send(number, tok_out.at[src_d, v], tok_out.at[src_d, v], p.cp)
+            piece = tok_out.at[src_d, p.from_y(j) * 2 + p.c]
+            q.arrived(y0 + slot * (p.Y - 1) + j - 1, piece)
+            q.send(c0 + slot * p.Y + j, piece, piece, p.cp)
+    g2.step_x()
     for gather in gathers:
-        gather.step_y()
+        gather.step_c()
     for slot in range(n_dp):
         src_d = lax.rem(p.d + n_dp - slot, n_dp)
         for j in range(p.Y):
-            v = p.from_y(j) * 2 + 1 - p.c
-            q.arrived(base + n_dp * (p.Y - 1) + slot * p.Y + j, tok_out.at[src_d, v])
-    for gather in gathers:
-        gather.step_c()
+            q.arrived(c0 + slot * p.Y + j, tok_out.at[src_d, p.from_y(j) * 2 + 1 - p.c])
     q.finish()
-    for copy in locals_[1:]:
-        copy.wait()
-
-
-def gather_weights(blocks, packed, n_dp, n_v):
-    groups = blocks.shape[0] // n_v
-    count = groups * Gather.count(n_dp, n_v) + (n_dp - 1) + n_dp * (n_v // 2 - 1) + n_dp * (n_v // 2)
+    own.wait()
+    local.wait()
+
+
+def run_front(blocks, table, ints, cap, n_dp, n_v):
+    f32, bf = jnp.float32, jnp.bfloat16
+    count = 3 * Gather.count(n_dp, n_v) + 2 * (n_dp - 1) + n_dp * (n_v - 1)
+    hbm = pl.BlockSpec(memory_space=pl.ANY)
+    vmem = pl.BlockSpec(memory_space=pltpu.VMEM)
+    wide = ceil_to(SEGS * SEG, 128)
+    rows = table.shape[0]
     return pl.pallas_call(
-        functools.partial(weights_kernel, n_dp, n_v),
+        functools.partial(front_kernel, n_dp, n_v, cap),
         out_shape=(
-            jax.ShapeDtypeStruct((n_dp,) + blocks.shape, blocks.dtype),
-            jax.ShapeDtypeStruct((n_dp, n_v) + packed.shape[1:], packed.dtype),
+            jax.ShapeDtypeStruct((n_dp,) + blocks.shape, bf),
+            jax.ShapeDtypeStruct((n_dp, n_v, cap, D), bf),
+            jax.ShapeDtypeStruct((n_dp,) + ints.shape, ints.dtype),
+            jax.ShapeDtypeStruct((n_dp * cap, rows), bf),
+            jax.ShapeDtypeStruct((n_dp, wide), f32),
+            jax.ShapeDtypeStruct((8, 128), f32),
         ),
-        in_specs=[pl.BlockSpec(memory_space=pl.ANY)] * 2,
-        out_specs=(pl.BlockSpec(memory_space=pl.ANY),) * 2,
+        in_specs=[hbm, vmem, vmem],
+        out_specs=(hbm, hbm, vmem, vmem, vmem, vmem),
         scratch_shapes=[
+            pltpu.VMEM((n_dp, cap, D), bf),
+            pltpu.VMEM((8 * n_dp * n_v, wide), bf),
+            pltpu.VMEM((wide, wide), bf),
             pltpu.SemaphoreType.DMA((count,)),
             pltpu.SemaphoreType.DMA((count,)),
             pltpu.SemaphoreType.DMA((2,)),
         ],
-        compiler_params=pltpu.CompilerParams(collective_id=0, has_side_effects=True),
-    )(blocks, packed)
-
-
-def ints_kernel(n_dp, in_ref, out_ref, ss, rs):
-    d, v = lax.axis_index("dp"), lax.axis_index("vocab")
-    sem = pltpu.get_barrier_semaphore()
-    for k in range(1, n_dp):
-        partner = (lax.rem(d + k, n_dp), v)
-        pl.semaphore_signal(sem, 1, device_id=partner, device_id_type=MESH)
-    pl.semaphore_wait(sem, n_dp - 1)
-    q = Copies((d, v), ss, rs)
-    for k in range(1, n_dp):
-        q.send(k - 1, in_ref, out_ref.at[d], (lax.rem(d + k, n_dp), v))
-    out_ref[d] = in_ref[...]
-    for k in range(1, n_dp):
-        q.arrived(k - 1, out_ref.at[lax.rem(d + n_dp - k, n_dp)])
-    q.finish()
-
-
-def gather_ints(values, n_dp):
-    return pl.pallas_call(
-        functools.partial(ints_kernel, n_dp),
-        out_shape=jax.ShapeDtypeStruct((n_dp,) + values.shape, values.dtype),
-        in_specs=[pl.BlockSpec(memory_space=pltpu.VMEM)],
-        out_specs=pl.BlockSpec(memory_space=pltpu.VMEM),
-        scratch_shapes=[pltpu.SemaphoreType.DMA((n_dp - 1,)), pltpu.SemaphoreType.DMA((n_dp - 1,))],
-        compiler_params=pltpu.CompilerParams(collective_id=1, has_side_effects=True),
-    )(values)
+        compiler_params=pltpu.CompilerParams(
+            collective_id=0, has_side_effects=True, vmem_limit_bytes=48 << 20
+        ),
+    )(blocks, table, ints)
 
 
 def head_kernel(
@@ -476,61 +521,124 @@
     )(layer, small, table)
 
 
-def adam_kernel(rates, scal_ref, *refs):
-    n = len(rates)
-    grads, ins, outs = refs[:n], refs[n : 4 * n], refs[4 * n : 7 * n]
-    bufs, sem_i, sem_o = refs[7 * n : 10 * n], refs[10 * n], refs[10 * n + 1]
+def adam_kernel(n_dp, cuts, scal_ref, table_g, block_g, small_g, *refs):
+    f32 = jnp.float32
+    n = 7
+    ins, outs, bufs = refs[: 3 * n], refs[3 * n : 6 * n], refs[6 * n : 9 * n]
+    up_g, ext_g, bias_g, sem_i, sem_o = refs[9 * n :]
     loads = [pltpu.make_async_copy(ins[k], bufs[k], sem_i.at[k]) for k in range(3 * n)]
     for copy in loads:
         copy.start()
     coef, one_hat, two_hat = scal_ref[0], scal_ref[1], scal_ref[2]
+    rb, width = block_g.shape[1:]
     stores = []
-    for i, rate in enumerate(rates):
+
+    def change(i, at, cols, grad, rate=LR_BIG):
         master, first, second = bufs[3 * i : 3 * i + 3]
+        g = grad.astype(f32) * coef
+        one = BETA_ONE * first[at, cols] + (1.0 - BETA_ONE) * g
+        two = BETA_TWO * second[at, cols] + (1.0 - BETA_TWO) * g * g
+        old = master[at, cols]
+        first[at, cols] = one
+        second[at, cols] = two
+        move = one * one_hat / (jnp.sqrt(two * two_hat) + ADAM_EPS) + DECAY * old
+        master[at, cols] = old - rate * move
+
+    def begin(i):
         for copy in loads[3 * i : 3 * i + 3]:
             copy.wait()
-        rows = master.shape[0]
-        chunk = 32 if rows % 32 == 0 else rows
-
-        def update(c, _, i=i, rate=rate, master=master, first=first, second=second, chunk=chunk):
-            at = pl.ds(c * chunk if isinstance(c, int) else pl.multiple_of(c * chunk, chunk), chunk)
-            g = grads[i][at, :].astype(jnp.float32) * coef
-            one = BETA_ONE * first[at, :] + (1.0 - BETA_ONE) * g
-            two = BETA_TWO * second[at, :] + (1.0 - BETA_TWO) * g * g
-            old = master[at, :]
-            move = one * one_hat / (jnp.sqrt(two * two_hat) + ADAM_EPS) + DECAY * old
-            first[at, :] = one
-            second[at, :] = two
-            master[at, :] = old - rate * move
-            return 0
-
-        if rows == chunk:
-            update(0, 0)
-        else:
-            lax.fori_loop(0, rows // chunk, update, 0)
+
+    def end(i):
         for k in range(3 * i, 3 * i + 3):
             copy = pltpu.make_async_copy(bufs[k], outs[k], sem_o.at[k])
             copy.start()
             stores.append(copy)
+
+    def chunks(rows, act):
+        size = 32 if rows % 32 == 0 else rows
+        if size == rows:
+            act(pl.ds(0, rows))
+        else:
+
+            def body(c, _):
+                act(pl.ds(pl.multiple_of(c * size, size), size))
+                return 0
+
+            lax.fori_loop(0, rows // size, body, 0)
+
+    every = slice(None)
+    begin(0)
+    chunks(bufs[0].shape[0], lambda at: change(0, at, every, table_g[at, :]))
+    end(0)
+    for i, blocks in ((1, range(3)), (2, range(3, 4))):
+        begin(i)
+        for j in blocks:
+            for s in range(cuts):
+                cols = pl.ds((j - blocks[0]) * D + s * width, width)
+                chunks(rb, lambda at: change(i, at, cols, block_g[j * cuts + s, at, :]))
+        end(i)
+    begin(3)
+    for j in range(4):
+        for s in range(cuts):
+            block = block_g[(4 + j) * cuts + s].astype(f32)
+            for d in range(n_dp // cuts):
+                to = (s * (n_dp // cuts) + d) * 4 * rb + j * rb
+                up_g[:, to : to + rb] = block[:, d * rb : (d + 1) * rb]
+    chunks(rb, lambda at: change(3, at, every, up_g[at, :]))
+    end(3)
+    begin(4)
+    for j in range(4):
+        for s in range(cuts):
+            cols = pl.ds(s * width, width)
+
+            def down(at, j=j, s=s, cols=cols):
+                change(4, pl.ds(j * rb + at.start, at.size), cols, block_g[(8 + j) * cuts + s, at, :])
+
+            chunks(rb, down)
+    end(4)
+    ext_g[...] = small_g[: ext_g.shape[0], :].astype(f32)
+    begin(5)
+    done = EXT // 8 * 8
+    for at in (pl.ds(0, done // 2), pl.ds(done // 2, done // 2), pl.ds(done, EXT - done)):
+        change(5, at, every, ext_g[at, :], LR_SMALL)
+    end(5)
+    begin(6)
+    for j in range(4):
+        for d in range(n_dp):
+            piece = ext_g[EXT + 5 + j : EXT + 6 + j, d * rb : (d + 1) * rb]
+            bias_g[:, d * 4 * rb + j * rb : d * 4 * rb + (j + 1) * rb] = piece
+    for k in range(12):
+        if 5 <= k < 9:
+            grad = bias_g[:, (k - 5) * D : (k - 4) * D]
+        else:
+            grad = ext_g[EXT + k : EXT + k + 1, :]
+        change(6, every, pl.ds(k * D, D), grad, LR_SMALL)
+    end(6)
     for copy in stores:
         copy.wait()
 
 
-def run_adam(scalars, grads, states, rates):
+def run_adam(scalars, table_g, block_g, small_g, states, n_dp, cuts):
     hbm = pl.BlockSpec(memory_space=pl.ANY)
-    n = len(rates)
+    vmem = pl.BlockSpec(memory_space=pltpu.VMEM)
     flat = [array for state in states for array in state]
+    n = len(flat)
+    rb = block_g.shape[1]
     return pl.pallas_call(
-        functools.partial(adam_kernel, rates),
+        functools.partial(adam_kernel, n_dp, cuts),
         out_shape=[jax.ShapeDtypeStruct(a.shape, a.dtype) for a in flat],
-        in_specs=[pl.BlockSpec(memory_space=pltpu.SMEM)]
-        + [pl.BlockSpec(memory_space=pltpu.VMEM)] * n
-        + [hbm] * (3 * n),
-        out_specs=[hbm] * (3 * n),
+        in_specs=[pl.BlockSpec(memory_space=pltpu.SMEM), vmem, vmem, vmem] + [hbm] * n,
+        out_specs=[hbm] * n,
         scratch_shapes=[pltpu.VMEM(a.shape, a.dtype) for a in flat]
-        + [pltpu.SemaphoreType.DMA((3 * n,)), pltpu.SemaphoreType.DMA((3 * n,))],
+        + [
+            pltpu.VMEM((rb, FF), jnp.float32),
+            pltpu.VMEM((ceil_to(EXT + 12, 16), D), jnp.float32),
+            pltpu.VMEM((1, FF), jnp.float32),
+            pltpu.SemaphoreType.DMA((n,)),
+            pltpu.SemaphoreType.DMA((n,)),
+        ],
         compiler_params=pltpu.CompilerParams(vmem_limit_bytes=56 << 20),
-    )(scalars, *grads, *flat)
+    )(scalars, table_g, block_g, small_g, *flat)
 
 
 def grads_kernel(n_dp, n_v, g_ref, e_ref, t_ref, g_out, e_out, t_out, bx, px, bz, ebx, epx, ebz, ss, rs, ls):
@@ -677,7 +785,7 @@
 
 
 def forward_kernel(
-    w_hbm, tok_ref, row_ref, col_ref, reset_ref, vec_ref, ext_ref, pos_ref,
+    w_hbm, tok_ref, slot_ref, row_ref, col_ref, reset_ref, vec_ref, ext_ref, pos_ref,
     x_o, hc_o, proj_o, p_o, one_o, mid_o, gp_o, act_o, two_o, chosen_o,
     w, x, hc, proj, probs, one, mid, gp, act, two, mask, hid, final, sem_w, sem_o,
 ):
@@ -708,7 +816,9 @@
     low_half = lane < HD
     for seg in range(SEGS):
         rows = pl.ds(seg * ROWS, ROWS)
-        x[seg] = tok_ref[rows, :].astype(f32) + ext_ref[:ROWS, :]
+        held = lax.broadcasted_iota(jnp.int32, (1, tok_ref.shape[0]), 1).astype(f32)
+        onehot = (slot_ref[rows, :] == held).astype(f32).astype(bf)
+        x[seg] = dot(onehot, tok_ref[...]) + ext_ref[:ROWS, :]
         x[seg, ROWS - MEM :, :] += ext_ref[ROWS + MEM : ROWS + 2 * MEM, :]
         first = ext_ref[ROWS : ROWS + MEM, :]
         if seg == 0:
@@ -773,7 +883,7 @@
         copy.wait()
 
 
-def run_forward(w_all, tok, marks, reset, vec, ext, pos):
+def run_forward(w_all, tok, slot, marks, reset, vec, ext, pos):
     f32, bf = jnp.float32, jnp.bfloat16
     n = SEGS * ROWS
     saved = [
@@ -793,7 +903,7 @@
         forward_kernel,
         out_shape=[jax.ShapeDtypeStruct(s, k) for s, k in saved]
         + [jax.ShapeDtypeStruct((MLM_PAD, D), bf)],
-        in_specs=[hbm, vmem, vmem, vmem, pl.BlockSpec(memory_space=pltpu.SMEM), vmem, vmem, vmem],
+        in_specs=[hbm] + [vmem] * 4 + [pl.BlockSpec(memory_space=pltpu.SMEM), vmem, vmem, vmem],
         out_specs=[hbm] * len(saved) + [vmem],
         scratch_shapes=[pltpu.VMEM((12, w_all.shape[0]) + w_all.shape[2:], bf)]
         + [pltpu.VMEM(s, k) for s, k in saved]
@@ -805,7 +915,7 @@
             pltpu.SemaphoreType.DMA((SEGS * 10,)),
         ],
         compiler_params=pltpu.CompilerParams(vmem_limit_bytes=60 << 20),
-    )(w_all, tok, marks[:, None, :], marks[:, :, None], reset, vec, ext, pos[:, None])
+    )(w_all, tok, slot[:, None], marks[:, None, :], marks[:, :, None], reset, vec, ext, pos[:, None])
 
 
 def backward_kernel(
@@ -1057,54 +1167,31 @@
         )
         return full.reshape(12, rb, cuts, width).transpose(0, 2, 1, 3).reshape(12 * cuts, rb, width)
 
-    def from_blocks(blocks):
-        full = blocks.reshape(12, cuts, rb, width).transpose(0, 2, 1, 3).reshape(12, rb, D)
-        return (
-            full[:3].transpose(1, 0, 2).reshape(1, rb, 3 * D),
-            full[3:4],
-            full[4:8].reshape(4, rb, n_dp, rb).transpose(1, 2, 0, 3).reshape(1, rb, FF),
-            full[8:].reshape(1, 4 * rb, D),
-        )
-
     ints = jnp.concatenate([ids[0], mlm_label[0]])[None]
     ints = jnp.pad(ints, ((0, 0), (0, ceil_to(ints.shape[1], 128) - ints.shape[1])), constant_values=-1)
-    ints_all = gather_ints(ints, n_dp)[:, 0]
-    ids_all = ints_all[:, :tokens_n]
-    labels_all = ints_all[:, tokens_n : tokens_n + MLM]
-    labels_all = jnp.pad(labels_all, ((0, 0), (0, MLM_PAD - MLM)), constant_values=-1)
-    holder = ids_all // own_rows
-    local_row = ids_all % own_rows
-    order = jnp.arange(tokens_n, dtype=jnp.int32)
-    same = (holder[:, :, None] == holder[:, None, :]) & (order[None, :, None] > order[None, None, :])
-    rank = jnp.sum(same.astype(jnp.int32), axis=-1)
     cap = ceil_to(2 * tokens_n // (n_dp * n_v) + 2, 16)
-    overflow = jnp.max(rank) >= cap
-    mine = holder == d_idx * n_v + v_idx
-    places = jnp.arange(cap, dtype=jnp.int32)
-    hit = mine[:, None, :] & (rank[:, None, :] == places[None, :, None])
-    packed_row = jnp.sum(jnp.where(hit, local_row[:, None, :] + 1, 0), axis=-1) - 1
-    own_slots = jnp.arange(own_rows, dtype=jnp.int32)
-    pick = (packed_row.reshape(n_dp * cap)[:, None] == own_slots[None, :]).astype(bf)
     table = embed_master.astype(bf)
-    packed = jnp.dot(pick, table, preferred_element_type=f32).astype(bf).reshape(n_dp, cap, D)
-
     blocks = to_blocks(
         qkv_master.astype(bf), out_master.astype(bf), up_master.astype(bf), down_master.astype(bf)
     )
-    w_all, tok_all = gather_weights(blocks, packed, n_dp, n_v)
+    w_all, tok_all, ints_all, pick, slots, most = run_front(blocks, table, ints, cap, n_dp, n_v)
     if cuts > 1 or rb % 16:
         w_all = w_all.reshape(n_dp, 12, cuts, rb, width).transpose(1, 0, 3, 2, 4).reshape(1, 12, D, D)
-
-    my_holder = holder[d_idx]
-    my_rank = rank[d_idx]
-    slot = (my_holder * cap + my_rank).reshape(SEGS, SEG)
-    slot = jnp.pad(slot, ((0, 0), (MEM, MEM)), constant_values=-1).reshape(SEGS * ROWS)
+    ids_all = ints_all[:, 0, :tokens_n]
+    labels_all = ints_all[:, 0, tokens_n : tokens_n + MLM]
+    labels_all = jnp.pad(labels_all, ((0, 0), (0, MLM_PAD - MLM)), constant_values=-1)
+    overflow = most[0, 0] >= cap
+
+    def padded(values):
+        values = values.reshape((SEGS, SEG) + values.shape[1:])
+        edges = ((0, 0), (MEM, MEM)) + ((0, 0),) * (values.ndim - 2)
+        values = jnp.pad(values, edges, constant_values=-1)
+        return values.reshape((SEGS * ROWS,) + values.shape[2:])
+
+    slot = padded(lax.dynamic_index_in_dim(slots, d_idx, keepdims=False)[:tokens_n])
 
     def packed_tokens(_):
-        slots = jnp.arange(n_dp * n_v * cap, dtype=jnp.int32)
-        onehot = (slot[:, None] == slots[None, :]).astype(bf)
-        rows = tok_all.reshape(n_dp * n_v * cap, D)
-        return jnp.dot(onehot, rows, preferred_element_type=f32).astype(bf)
+        return tok_all.reshape(n_dp * n_v * cap, D), slot
 
     def whole_tokens(_):
         whole = lax.all_gather(table, "dp", axis=0, tiled=True)
@@ -1112,9 +1199,10 @@
         row_ids = (at // own_rows * n_v + v_idx) * own_rows + at % own_rows
         onehot = (ids[0][:, None] == row_ids[None, :]).astype(bf)
         rows = lax.psum(jnp.dot(onehot, whole, preferred_element_type=f32).astype(bf), "vocab")
-        return jnp.pad(rows.reshape(SEGS, SEG, D), ((0, 0), (MEM, MEM), (0, 0))).reshape(-1, D)
-
-    tokens = lax.cond(overflow, whole_tokens, packed_tokens, 0)
+        rows = jnp.pad(rows, ((0, n_dp * n_v * cap - tokens_n), (0, 0)))
+        return rows, padded(jnp.arange(tokens_n, dtype=jnp.int32).astype(f32))
+
+    token_rows, token_slot = lax.cond(overflow, whole_tokens, packed_tokens, 0)
     marks = jnp.pad(docs.reshape(SEGS, SEG), ((0, 0), (MEM, MEM)), constant_values=-1)
     vec = vectors_master[0].reshape(12, D)
     b_up = vec[5:9].reshape(n_dp, 4, rb).transpose(1, 0, 2).reshape(4, D)
@@ -1122,7 +1210,7 @@
     positions = mlm_pos[0]
     at_rows = positions // SEG * ROWS + MEM + positions % SEG
     at_rows = jnp.concatenate([at_rows, jnp.full((MLM_PAD - MLM,), -1, jnp.int32)])
-    *saved, chosen = run_forward(w_all, tokens, marks, resets[0], vec, extras_master, at_rows)
+    *saved, chosen = run_forward(w_all, token_rows, token_slot, marks, resets[0], vec, extras_master, at_rows)
     rows_v = MLM_PAD // n_v
     d_chosen, d_table, loss = run_head(chosen.reshape(n_v, rows_v, D), table, labels_all, n_dp, n_v)
     loss = loss[0, 0]
@@ -1130,7 +1218,7 @@
     small_rows = EXT + 12
     e_rows = ceil_to(-(-small_rows // (n_dp * n_v)), 16)
     at = jnp.arange(n_dp * cap, dtype=jnp.int32)
-    give = (at // cap * n_v + v_idx) * cap + at % cap
+    give = ((at // cap * n_v + v_idx) * cap + at % cap).astype(f32)
     shares, small, d_packed, d_tok = run_backward(
         w_all,
         saved,
@@ -1160,22 +1248,16 @@
     def whole_d_table(_):
         d_all = d_tok.reshape(SEGS, ROWS, D)[:, MEM : MEM + SEG].reshape(tokens_n, D)
         d_all = lax.all_gather(d_all, "dp", axis=0, tiled=True)
-        row_ids = (d_idx * n_v + v_idx) * own_rows + own_slots
+        row_ids = (d_idx * n_v + v_idx) * own_rows + jnp.arange(own_rows, dtype=jnp.int32)
         onehot = (ids_all.reshape(-1)[:, None] == row_ids[None, :]).astype(bf)
         return jnp.einsum("tv,td->vd", onehot, d_all, preferred_element_type=f32)
 
     s_table = d_table + lax.cond(overflow, whole_d_table, packed_d_table, 0)
     small_all = small_all.reshape(n_dp * n_v * e_rows, D)
-    norm = jnp.sqrt(run_norm(g_blocks, small_all[:small_rows], s_table, n_dp, n_v)[0, 0])
-    s_qkv, s_out, s_up, s_down = (grad[0] for grad in from_blocks(g_blocks))
-    g_ext = small_all[:EXT].astype(f32)
-    g_vec = small_all[EXT:small_rows].astype(f32)
-    g_up_bias = g_vec[5:9].reshape(4, n_dp, rb).transpose(1, 0, 2).reshape(4, D)
-    g_vec = jnp.concatenate([g_vec[:5], g_up_bias, g_vec[9:]])
+    norm = jnp.sqrt(run_norm(g_blocks, small_all, s_table, n_dp, n_v)[0, 0])
     coef = jnp.minimum(1.0, CLIP / (norm + 1e-06))
     t = step[0].astype(f32)
     scalars = jnp.stack([coef, 1.0 / (1.0 - BETA_ONE**t), 1.0 / (1.0 - BETA_TWO**t)])
-    wide = (12, D)
     states = (
         (embed_master, embed_first, embed_second),
         (qkv_master[0], qkv_first[0], qkv_second[0]),
@@ -1183,17 +1265,11 @@
         (up_master[0], up_first[0], up_second[0]),
         (down_master[0], down_first[0], down_second[0]),
         (extras_master, extras_first, extras_second),
-        (vectors_master.reshape(wide), vectors_first.reshape(wide), vectors_second.reshape(wide)),
+        (vectors_master, vectors_first, vectors_second),
     )
-    new = run_adam(
-        scalars,
-        (s_table, s_qkv, s_out, s_up, s_down, g_ext, g_vec),
-        states,
-        (LR_BIG, LR_BIG, LR_BIG, LR_BIG, LR_BIG, LR_SMALL, LR_SMALL),
-    )
+    new = run_adam(scalars, s_table, g_blocks, small_all, states, n_dp, cuts)
     layer = [value[None] for value in new[3:15]]
-    vectors = [value.reshape(vectors_master.shape) for value in new[18:]]
-    return (loss, norm, *layer, *new[:3], *vectors, *new[15:18])
+    return (loss, norm, *layer, *new[:3], *new[18:], *new[15:18])
 
 
 def solution(mesh):

time: 450 us -> 394 us (0.88)
  Pallas kernels: 364 us -> 346 us
  local copies, waits for them, and re-layouts: 26.8 us -> 13.7 us
  other arithmetic: 18 us -> 6.44 us
  loops' own time: 9.11 us -> 0.74 us
  matrix products: 5.76 us -> 0.57 us
    pallas_call x3 -> x2, Pallas kernels: 131 us -> 113 us  [the longest x1 97 us: run_front(): pl.pallas_call(functools.partial(front_kernel, n_dp, n_v, cap), out_shape...]
    another operation x1, loops' own time: 8.84 us -> 0.47 us  [per_device(): token_rows, token_slot = lax.cond(overflow, whole_tokens, packed_tokens, 0)]
    dot_general x2 -> x0, matrix products: 5.19 us -> none  [the longest x1 3.84 us: packed_tokens(): return jnp.dot(onehot, rows, preferred_element_type=f32).astype(bf)]
    reduce_sum x2 -> x0, other arithmetic: 4.79 us -> none  [the longest x1 4.41 us: per_device(): rank = jnp.sum(same.astype(jnp.int32), axis=-1)]
where the time goes in v3:
time: 394 us; the launch traced here: 386 us
  Pallas kernels  346 us (88%)
  between operations  18.8 us (5%)
  local copies, waits for them, and re-layouts  13.7 us (3%)
  other arithmetic  6.44 us (2%)
    pallas_call x1, Pallas kernels, run_front(): pl.pallas_call(functools.partial(front_kernel, n_dp, n_v, cap), out_shape...  97 us
    pallas_call x1, Pallas kernels, reduce_grads(): pl.pallas_call(functools.partial(grads_kernel, n_dp, n_v), out_shape=(jax...  82.8 us
    pallas_call x1, Pallas kernels, run_head(): pl.pallas_call(functools.partial(head_kernel, n_dp, n_v), out_shape=[jax....  58.1 us
    pallas_call x1, Pallas kernels, run_backward(): pl.pallas_call(functools.partial(backward_kernel, cuts), out_shape=[jax.S...  45.2 us
    pallas_call x1, Pallas kernels, run_forward(): pl.pallas_call(forward_kernel, out_shape=[jax.ShapeDtypeStruct(s, k) for...  36.3 us
    pallas_call x1, Pallas kernels, run_adam(): pl.pallas_call(functools.partial(adam_kernel, n_dp, cuts), out_shape=[jax...  16.1 us
    pallas_call x1, Pallas kernels, run_norm(): pl.pallas_call(functools.partial(norm_kernel, n_dp, n_v), out_shape=jax.S...  10.2 us

profile of v3, /device:TPU:0, one launch (start us, length us, event | category | flops | bytes accessed | tf_op | source)
XLA Modules:
  0.0 386.0 jit_solution(13663643524262656971)
XLA Ops:
  7.2 1.4 convert_element_type.58
  8.9 0.8 reshape_squeeze.12
  9.8 0.6 reshape.222
  11.4 1.2 copy-done.3
  12.6 0.9 convert_element_type.59.table_ref
  13.7 97.0 %shard_map.434 = (bf16[8,12,96,768]{3,2,1,0:T(8,128)(2,1)}, bf16[8,4,48,768]{3,2,1,0:T(8,128)(2,1)}, s32[8,1,896]{2,1,0:T(1,128)S(1)}, bf16[384,480]{1,0:T(8,128...) custom-call(bf16[12,96,768]{2,1,0:T(8,128)(2,1)S(1)} %pad_maximum_fusion.w_ref, ...), custom_call_target="tpu_custom_call" | custom-call | tf_op jit(solution)/shard_map/pallas_call | solution.py:297
  112.6 0.9 copy.79
  114.3 0.9 copy.70.col_ref
  116.2 0.6 pad_maximum_fusion.1.vec_ref
  116.9 0.7 copy.71.pos_ref
  117.6 36.3 %shard_map.435 = (f32[2,384,768]{2,1,0:T(8,128)}, bf16[2,768,768]{2,1,0:T(8,128)(2,1)}, bf16[3,768,768]{2,1,0:T(8,128)(2,1)}, bf16[2,12,384,384]{3,2,1,0:T(8,128...) custom-call(bf16[8,12,96,768]{3,2,1,0:T(8,128)(2,1)} %get-tuple-elem, ...), custom_call_target="tpu_custom_call" | custom-call | tf_op jit(solution)/shard_map/pallas_call | solution.py:902
  154.0 0.6 pad.31.tags_ref
  154.6 58.1 %shard_map.436 = (bf16[4,32,768]{2,1,0:T(8,128)(2,1)}, f32[480,768]{1,0:T(8,128)}, f32[8,128]{1,0:T(8,128)}) custom-call(bf16[4,32,768]{2,1,0:T(8,128)(2,1)} %bitcast.117, bf16[480,768]{1,0:T(8,128)(2,1)} %convert_element_type.59.table_ref, s32[1,1024]{1,0:T(1,128)} %bitcast.119, s32[8,128]{1,0:T(8,128)} %pad.31.tags_ref), custom_call_target="tpu_custom_call" | custom-call | tf_op jit(solution)/shard_map/pallas_call | solution.py:434
  212.7 1.2 slice.47
  213.9 0.8 fusion.32.give_ref
  215.3 45.2 %shard_map.437 = (bf16[3,768,768]{2,1,0:T(8,128)(2,1)}, f32[424,768]{1,0:T(8,128)}, bf16[384,768]{1,0:T(8,128)(2,1)}, bf16[768,768]{1,0:T(8,128)(2,1)}) custom-call(bf16[8,12,96,768]{3,2,1,0:T(8,128)(2,1)} %get-tuple-element.112.w_hbm, f32[2,384,768]{2,1,0:T(8,128)} %get-tuple-element.121.x_i, bf16[2,768,768]{2,1,0:T(8,128)(2,1)} %get-tuple-element.122.hc_i, ...), custom_call_target="tpu_custom_call" | custom-call | tf_op jit(solution)/shard_map/pallas_call | solution.py:1080
  260.5 1.4 convert_element_type.63
  262.0 0.7 dynamic-slice_bitcast_fusion.e_ref
  262.7 82.8 %shard_map.438 = (bf16[12,96,768]{2,1,0:T(8,128)(2,1)}, bf16[8,4,16,768]{3,2,1,0:T(8,128)(2,1)}, bf16[8,48,768]{2,1,0:T(8,128)(2,1)S(1)}) custom-call(bf16[3,4,2,96,768]{4,3,2,1,0:T(8,128)(2,1)} %bitcast.96, bf16[4,2,16,768]{3,2,1,0:T(8,128)(2,1)} %dynamic-slice_bitcast_fusion.e_ref, bf16[8,48,768]{2,1,0:T(8,128)(2,1)} %bitcast.113), custom_call_target="tpu_custom_call" | custom-call | tf_op jit(solution)/shard_map/pallas_call | solution.py:727
  345.5 0.8 conditional.3
  347.1 1.3 copy-done.1
  348.5 10.2 %shard_map.439 = f32[8,128]{1,0:T(8,128)S(1)} custom-call(bf16[12,96,768]{2,1,0:T(8,128)(2,1)S(1)} %copy-done.1, bf16[512,768]{1,0:T(8,128)(2,1)S(1)} %bitcast.93, f32[480,768]{1,0:T(8,128)S(1)} %add.148.table_ref.table_g), custom_call_target="tpu_custom_call" | custom-call | tf_op jit(solution)/shard_map/pallas_call | solution.py:507
  360.8 0.7 pad_maximum_fusion.2.scal_ref
  361.5 16.1 %shard_map.440 = (f32[480,768]{1,0:T(8,128)}, f32[480,768]{1,0:T(8,128)}, f32[480,768]{1,0:T(8,128)}, f32[96,2304]{1,0:T(8,128)}, f32[96,2304]{1,0:T(8,128)}, /*...) custom-call(f32[3]{0:T(128)} %pad_maximum_fusion.2.scal_ref, ...), custom_call_target="tpu_custom_call" | custom-call | tf_op jit(solution)/shard_map/pallas_call | solution.py:627
  (66 shorter events, 6.4 us)
Async XLA Ops:
  7.2 1.6 copy-start.4
  9.7 1.0 copy-start.7
  9.7 1.3 copy-start.5
  11.2 1.4 copy-start.3
  12.6 0.9 copy-start.12
  12.6 1.0 copy-start.14
  110.7 43.2 %copy-start.10 = (s32[8,1,896]{2,1,0:T(1,128)}, s32[8,1,896]{2,1,0:T(1,128)S(1)}, u32[]{:S(2)}) copy-start(s32[8,1,896]{2,1,0:T(1,128)S(1)} %get-tuple-element.119) | copy-start | bytes 86020
  112.1 1.4 copy-start.13
  112.1 3.8 copy-start.9
  112.1 4.8 %copy-start.15 = (s32[1,112]{1,0:T(1,128)S(1)}, s32[1,112]{1,0:T(1,128)}, u32[]{:S(2)}) copy-start(s32[1,112]{1,0:T(1,128)} %param.34) | copy-start | bytes 1348
  262.7 82.8 %copy-start.8 = (bf16[384,480]{1,0:T(8,128)(2,1)S(1)}, bf16[384,480]{1,0:T(8,128)(2,1)}, u32[]{:S(2)}) copy-start(bf16[384,480]{1,0:T(8,128)(2,1)} %get-tuple-element.138) | copy-start | bytes 1105924
  345.5 1.4 copy-start.6
  346.9 1.5 copy-start.1
  346.9 1.7 copy-start.2
  348.5 10.2 %copy-start = (f32[480,768]{1,0:T(8,128)}, f32[480,768]{1,0:T(8,128)S(1)}, u32[]{:S(2)}) copy-start(f32[480,768]{1,0:T(8,128)S(1)} %add.148.table_ref.table_g) | copy-start | bytes 4423684
